TPU v7x, 256 devices: a whole 4x4x8 slice. The times are simulated.
256 devices in a mesh: ta: 2 (over y_lo), gx: 128 (over y_hi, z, x, core).
Axes of the slice: x: 4, y: 4 (y_hi: 2, y_lo: 2; y = y_hi * 2 + y_lo), z: 8, core: 2. Of those that a mesh axis runs over, the one named last changes fastest.
Arguments:
- modes: bfloat16 [12, 96, 131072], P('ta', None, 'gx'), parts along dimension 0, may hold values from -6 to 6
- links: float32 [6, 18, 131072], P('ta', None, 'gx'), parts along dimension 0, may hold values from -2.5 to 2.5
- sites: int32 [6144], P(('ta', 'gx')), parts along dimension 0, may hold values from 0 to 1023, as said below
- counts: int32 [256], P(('ta', 'gx')), parts along dimension 0, may hold values from 1 to 24, as said below
- pair_table: int32 [9216], P('gx'), may hold values from 0 to 9215, each once
Outputs:
- elementals: float32 [18432, 192], P(('ta', 'gx')), parts along dimension 0
There are 2 independent parts, one for each index of `ta`. A program takes and returns all parts, laid end to end along the dimension named above; an argument that names none is the same for every part. Nothing has to cross between parts.
Inputs may be any that keep to these rules, and one draw needn't show every extreme that they name: `counts`: some device has all 24 slots live. `sites`: the first slot of every device lists a site in that device's last x-plane.
All inputs are finite; a program needn't handle non-finite values.
Results may differ from a plain program's by a relative error of at most 0.0057.
Values may be sent and summed in bfloat16 or wider, within the bound.
No kernel may reach another device: no remote copies, remote signals or barrier semaphores. Data moves between devices by JAX's collectives and lax.ppermute only.
A program may use at most 128 MiB of HBM per device.

v0:
```python
import jax
import jax.numpy as jnp
from jax import lax
from jax.sharding import PartitionSpec as P

MODES = 96
LY = 16
LZ = 16


def shifted(value, axis, steps):
    count = lax.axis_size(axis)
    pairs = [(source, (source + steps) % count) for source in range(count)]
    return lax.ppermute(value, axis, pairs)


def build(field, links, at, near, live):
    panels = []
    for k in range(3):
        vec = field[:, :, near[k]].astype(jnp.float32)
        link = links[k][:, at]
        comps = []
        for i in range(3):
            real_part = jnp.zeros(vec.shape[1:], jnp.float32)
            imag_part = jnp.zeros(vec.shape[1:], jnp.float32)
            for j in range(3):
                link_re = link[(i * 3 + j) * 2]
                link_im = link[(i * 3 + j) * 2 + 1]
                real_part = real_part + link_re * vec[2 * j] - link_im * vec[2 * j + 1]
                imag_part = imag_part + link_re * vec[2 * j + 1] + link_im * vec[2 * j]
            comps.append(real_part)
            comps.append(imag_part)
        panels.append(jnp.where(live, jnp.stack(comps), 0.0).astype(jnp.bfloat16))
    return jnp.stack(panels)


def contract(panel, first, second):
    left = panel[0][:, first, :].astype(jnp.float32)
    right = panel[1][:, second, :].astype(jnp.float32)

    def cmul(i, j):
        return (
            left[2 * i] * right[2 * j] - left[2 * i + 1] * right[2 * j + 1],
            left[2 * i] * right[2 * j + 1] + left[2 * i + 1] * right[2 * j],
        )

    cross_re = []
    cross_im = []
    for i, j in ((1, 2), (2, 0), (0, 1)):
        plus = cmul(i, j)
        minus = cmul(j, i)
        cross_re.append(plus[0] - minus[0])
        cross_im.append(plus[1] - minus[1])
    w_re = jnp.stack(cross_re).astype(jnp.bfloat16)
    w_im = jnp.stack(cross_im).astype(jnp.bfloat16)
    third = panel[2]
    t_re = third[0::2]
    t_im = third[1::2]

    def inner(u, v):
        return jnp.einsum("cps,cms->pm", u, v, preferred_element_type=jnp.float32)

    return jnp.concatenate(
        [inner(w_re, t_re) - inner(w_im, t_im), inner(w_re, t_im) + inner(w_im, t_re)], axis=1
    )


def shards(modes, links, sites, counts, pair_table):
    plane = LY * LZ
    ahead = shifted(modes[:, :, :plane], "gx", -1)
    extended = jnp.concatenate([modes, ahead], axis=2)
    ycoord = sites // LZ % LY
    zcoord = sites % LZ
    base = sites - ycoord * LZ - zcoord
    near = [
        sites + plane,
        base + (ycoord + 1) % LY * LZ + zcoord,
        base + ycoord * LZ + (zcoord + 1) % LZ,
    ]
    live = jnp.arange(sites.shape[0], dtype=jnp.int32) < counts[0]
    panel = build(extended, links, sites, near, live)
    ndevices = lax.axis_size("gx")
    scale = 1.0 / jnp.sqrt(jnp.float32(ndevices * sites.shape[0]))
    first = pair_table // MODES
    second = pair_table % MODES
    total = contract(lax.all_gather(panel, "gx", axis=3, tiled=True), first, second)
    return total * scale


def solution(mesh):
    placed = (P("ta", None, "gx"), P("ta", None, "gx"), P(("ta", "gx")), P(("ta", "gx")), P("gx"))
    return jax.shard_map(
        shards, mesh=mesh, in_specs=placed, out_specs=P(("ta", "gx"), None), check_vma=False
    )
```

profile of v0, /device:TPU:2, one launch (start us, length us, event | category | flops | bytes accessed | tf_op | source)
XLA Modules:
  0.0 256.6 jit_solution(17403591975864865442)
XLA Ops:
  6.5 3.2 %copy.33 = bf16[6,96,1024]{1,0,2:T(8,128)(2,1)S(1)} copy(bf16[6,96,1024]{2,1,0:T(8,128)(2,1)} %param.5) | data formatting | bytes 2359296 | tf_op args[0]
  9.8 0.8 slice.515
  10.9 0.6 gather_fusion.4
  11.5 0.5 slice_reduce_fusion.5
  12.2 0.6 gather_fusion.2
  13.0 0.6 gather_fusion
  14.3 0.5 slice_reduce_fusion.23
  14.8 0.5 slice_reduce_fusion.41
  15.3 2.3 collective-permute-done
  17.6 7.6 %pad_maximum_fusion = bf16[6,96,1280]{1,0,2:T(8,128)(2,1)} fusion(bf16[6,96,256]{1,0,2:T(8,128)(2,1)S(1)} %collective-permute-done, bf16[6,96,1024]{1,0,2:T(8,128)(2,1)S(1)} %copy.33), kind=kLoop, calls=%fused_computation.10 | loop fusion | flops 737280 | bytes 2949120 | tf_op jit(solution)/shard_map/concatenate | solution.py:71
  25.2 2.3 gather_fusion.5
  28.1 2.3 gather_fusion.3
  31.0 2.3 gather_fusion.1
  34.1 0.7 pad_maximum_fusion.7
  34.8 153.8 %all-gather.2.cloned.1.call-done = bf16[3,6,96,3072]{2,3,1,0:T(8,128)(2,1)} async-done(((bf16[3,6,96,24]{2,3,1,0:T(8,128)(2,1)}), bf16[3,6,96,3072]{2,3,1,0:T(8,128)(2,1)}) %all-gather.2.cloned.1.call-update) | async-done | bytes 10616848 | tf_op jit(solution)/shard_map/all_gather | solution.py:86
  188.6 10.9 %fusion.37 = (bf16[1,6,96,3072]{2,3,1,0:T(8,128)(2,1)}, bf16[1,6,96,3072]{2,3,1,0:T(8,128)(2,1)}, bf16[1,6,96,3072]{2,3,1,0:T(8,128)(2,1)}) fusion(bf16[3,6,96,3072]{2,3,1,0:T(8,128)(2,1)} %all-gather.2.cloned.1.call-done), kind=kLoop, calls=%fused_computation.154 | loop fusion | bytes 21233664 | tf_op jit(solution)/shard_map/slice | solution.py:39
  199.4 9.0 %copy.48 = bf16[1,6,96,3072]{3,1,2,0:T(8,128)(2,1)} copy(bf16[1,6,96,3072]{2,3,1,0:T(8,128)(2,1)} %get-tuple-element.61) | data formatting | bytes 7077888
  208.4 3.1 %gather_fusion.7 = bf16[72,6,3072]{2,1,0:T(8,128)(2,1)S(1)} fusion(bf16[6,96,3072]{2,0,1:T(8,128)(2,1)} %bitcast.72, s32[1024]{0:T(1024)S(1)} %get-tuple-element.84), kind=kCustom, calls=%fused_computation.7 | custom fusion | bytes 5308704 | tf_op jit(solution)/shard_map/gather | solution.py:39
  211.5 3.9 %convert_bitcast_fusion = f32[6,72,3072]{2,1,0:T(8,128)} fusion(bf16[72,6,3072]{2,1,0:T(8,128)(2,1)S(1)} %gather_fusion.7), kind=kLoop, calls=%fused_computation.8 | loop fusion | flops 1327104 | bytes 7962624 | tf_op jit(solution)/shard_map/convert_element_type | solution.py:39
  215.4 9.0 %copy.47 = bf16[1,6,96,3072]{3,1,2,0:T(8,128)(2,1)} copy(bf16[1,6,96,3072]{2,3,1,0:T(8,128)(2,1)} %get-tuple-element.62) | data formatting | bytes 7077888
  224.4 5.3 %gather_fusion.6 = bf16[72,6,3072]{2,1,0:T(8,128)(2,1)} fusion(bf16[6,96,3072]{2,0,1:T(8,128)(2,1)} %bitcast.71, s32[1024]{0:T(1024)S(1)} %get-tuple-element.85), kind=kCustom, calls=%fused_computation.6 | custom fusion | bytes 5308704 | tf_op jit(solution)/shard_map/gather | solution.py:38
  229.8 3.7 %convert_bitcast_fusion.1 = f32[6,72,3072]{2,1,0:T(8,128)S(1)} fusion(bf16[72,6,3072]{2,1,0:T(8,128)(2,1)} %gather_fusion.6), kind=kLoop, calls=%fused_computation.9 | loop fusion | flops 1327104 | bytes 7962624 | tf_op jit(solution)/shard_map/convert_element_type | solution.py:38
  233.5 2.0 subtract_convert_fusion.5
  235.4 2.1 subtract_convert_fusion.3
  237.5 2.1 subtract_convert_fusion.1
  239.6 4.6 %copy.49 = bf16[1,6,96,3072]{3,2,1,0:T(8,128)(2,1)S(1)} copy(bf16[1,6,96,3072]{2,3,1,0:T(8,128)(2,1)} %get-tuple-element.63) | data formatting | bytes 7077888
  244.2 2.1 fusion.8
  246.3 0.7 fusion.11
  247.1 0.7 fusion.23
  247.8 0.3 copy-done
  248.4 0.7 fusion.20
  249.1 0.7 maximum_multiply_fusion
  (59 shorter events, 2.8 us)
Async XLA Ops:
  6.5 4.1 %copy-start.7 = (s32[24]{0:T(128)S(1)}, s32[24]{0:T(128)}, u32[]{:S(2)}) copy-start(s32[24]{0:T(128)} %param.7) | copy-start | bytes 292
  6.5 4.1 %copy-start.6 = (f32[3,18,1024]{2,1,0:T(8,128)S(1)}, f32[3,18,1024]{2,1,0:T(8,128)}, u32[]{:S(2)}) copy-start(f32[3,18,1024]{2,1,0:T(8,128)} %param.6) | copy-start | bytes 663556
  6.5 182.0 %all-gather.2.cloned.1.call-start = ((), (), s32[]{:S(2)}) async-start(), calls=%async_computation | async-start | bytes 14266368 | tf_op jit(solution)/shard_map/all_gather | solution.py:86
  10.6 7.0 %collective-permute-start = (bf16[6,96,256]{1,0,2:T(8,128)(2,1)}, bf16[6,96,256]{1,0,2:T(8,128)(2,1)S(1)}, u32[]{:S(2)}, u32[]{:S(2)}) collective-permute-start(bf16[6,96,256]{1,0,2:T(8,128)(2,1)} %slice.515), channel_id=1, source_target_pairs={{0,127},{1,0},{2,1},{3,2},{4,3},{5,4},{6,5},{7,6},{8,7},{9,8},{10,... | collective-permute-start | bytes 884744 | tf_op jit(solution)/shard_map/ppermute | solution.py:14
  25.2 9.5 %copy-start.8 = (s32[72]{0:T(128)S(1)}, s32[72]{0:T(128)}, u32[]{:S(2)}) copy-start(s32[72]{0:T(128)} %param.9) | copy-start | bytes 868
  224.4 9.0 %slice-start = ((s8[5308416]{0:T(1024)(128)(4,1)}), s8[1114112]{0:T(1024)(128)(4,1)S(1)}, s32[]{:S(2)}) async-start(s8[5308416]{0:T(1024)(128)(4,1)} %bitcast.69), calls=%async_computation.1 | async-start | bytes 2228224
  229.8 3.7 %slice-start.1 = ((s8[5308416]{0:T(1024)(128)(4,1)}), s8[4194304]{0:T(1024)(128)(4,1)S(1)}, s32[]{:S(2)}) async-start(s8[5308416]{0:T(1024)(128)(4,1)} %bitcast.69), calls=%async_computation.2 | async-start | bytes 8388608
  244.2 2.1 copy-start.3
  244.2 2.1 copy-start.4
  244.2 2.1 copy-start.5
  247.1 1.0 copy-start
  247.1 1.1 copy-start.1
  247.1 1.3 copy-start.2
Sparse Core Ops, SparseCore 0:
  34.9 153.6 all-gather.1
where the time goes:
time: 259 us; the launch traced here: 257 us
  waiting for transfers between devices  156 us (60%)
  local copies, waits for them, and re-layouts  57.4 us (22%)
  other arithmetic  24.5 us (9%)
  between operations  14.4 us (6%)
  matrix products  4.24 us (2%)
    all_gather x1, waiting for transfers between devices, shards(): lax.all_gather(panel, 'gx', axis=3, tiled=True)  154 us
    unnamed x29, local copies, waits for them, and re-layouts  27 us
    slice x1, local copies, waits for them, and re-layouts, contract(): right = panel[1][:, second, :].astype(jnp.float32)  10.9 us
    concatenate x1, other arithmetic, shards(): extended = jnp.concatenate([modes, ahead], axis=2)  7.58 us
    gather x3, local copies, waits for them, and re-layouts, build(): vec = field[:, :, near[k]].astype(jnp.float32)  6.98 us
    another operation x3, other arithmetic  6.09 us
    gather x1, local copies, waits for them, and re-layouts, contract(): left = panel[0][:, first, :].astype(jnp.float32)  5.34 us
  transfers between devices with their start and end apart: 2, of which 2 were waited for; matrix products, arithmetic and copies ran while one was open for 2% of the time, Pallas kernels for 0%

commit v1 on v0

v1 whole, which is shorter than its diff:
```python
import jax
import jax.numpy as jnp
from jax import lax
from jax.experimental import pallas as pl
from jax.experimental.pallas import tpu as pltpu
from jax.sharding import PartitionSpec as P

MODES = 96
LY = 16
LZ = 16
PLANE = LY * LZ
SITES = 1024
SLOTS = 24
ROWS = 72
NEAR = 8
FAR = 16
LANES = 128
KWIDE = 256
NEAR_GROUPS = [[NEAR * j + i for i in range(NEAR)] for j in range(FAR)]
FAR_GROUPS = [[NEAR * j + i for j in range(FAR)] for i in range(NEAR)]
PACKED = 112


def build_kernel(sites_ref, counts_ref, modes_ref, ahead_ref, links_ref, out_ref, rows_ref):
    lane = lax.broadcasted_iota(jnp.int32, (1, LANES), 1)
    slot = jnp.where(lane < SLOTS, lane, jnp.where(lane < 2 * SLOTS, lane - SLOTS, lane - 2 * SLOTS))
    site = jnp.zeros((1, LANES), jnp.int32)
    for s in range(SLOTS):
        site = jnp.where(slot == s, sites_ref[s], site)
    z = site & (LZ - 1)
    y = (site >> 4) & (LY - 1)
    base = site - (y << 4) - z
    near = jnp.where(
        lane < SLOTS,
        site + PLANE,
        jnp.where(
            lane < 2 * SLOTS,
            base + (((y + 1) & (LY - 1)) << 4) + z,
            base + (y << 4) + ((z + 1) & (LZ - 1)),
        ),
    )
    used = lane < 3 * SLOTS
    near = jnp.where(used, near, -1)
    at = jnp.where(used, site, -1)
    row = lax.broadcasted_iota(jnp.int32, (SITES, LANES), 0)
    pick = jnp.where(row == near, 1.0, 0.0).astype(jnp.bfloat16)
    pick_ahead = jnp.where(row[:PLANE] + SITES == near, 1.0, 0.0).astype(jnp.bfloat16)
    pick_site = jnp.where(row == at, 1.0, 0.0).astype(jnp.bfloat16)

    field = modes_ref[...].reshape(6 * MODES, SITES)
    ahead = ahead_ref[...].reshape(6 * MODES, PLANE)
    vec = jnp.dot(field, pick, preferred_element_type=jnp.float32) + jnp.dot(
        ahead, pick_ahead, preferred_element_type=jnp.float32
    )

    rows_ref[...] = jnp.zeros_like(rows_ref)
    for k in range(3):
        rows_ref[24 * k : 24 * k + 18, :] = links_ref[k]
    exact = rows_ref[...]
    high = exact.astype(jnp.bfloat16).astype(jnp.float32)
    rest = exact - high
    middle = rest.astype(jnp.bfloat16).astype(jnp.float32)
    low = rest - middle
    split = jnp.concatenate([high, middle, low], axis=0).astype(jnp.bfloat16)
    found = jnp.dot(split, pick_site, preferred_element_type=jnp.float32)
    found = found[0:72] + found[72:144] + found[144:216]
    link = jnp.where(
        lane < SLOTS, found[0:24], jnp.where(lane < 2 * SLOTS, found[24:48], found[48:72])
    )

    live = slot < counts_ref[0]
    turned = []
    for i in range(3):
        real_part = jnp.zeros((MODES, LANES), jnp.float32)
        imag_part = jnp.zeros((MODES, LANES), jnp.float32)
        for j in range(3):
            at_ij = (i * 3 + j) * 2
            link_re = link[at_ij : at_ij + 1]
            link_im = link[at_ij + 1 : at_ij + 2]
            vec_re = vec[2 * j * MODES : (2 * j + 1) * MODES]
            vec_im = vec[(2 * j + 1) * MODES : (2 * j + 2) * MODES]
            real_part = real_part + link_re * vec_re - link_im * vec_im
            imag_part = imag_part + link_re * vec_im + link_im * vec_re
        turned.append(jnp.where(live, real_part, 0.0).T)
        turned.append(jnp.where(live, imag_part, 0.0).T)
    panel = [turned[c][k * SLOTS : (k + 1) * SLOTS] for k in range(3) for c in range(6)]
    out_ref[...] = jnp.concatenate(panel, axis=0).astype(jnp.bfloat16)


def build(sites, counts, modes, ahead, links):
    smem = pl.BlockSpec(memory_space=pltpu.SMEM)
    vmem = pl.BlockSpec(memory_space=pltpu.VMEM)
    return pl.pallas_call(
        build_kernel,
        out_shape=jax.ShapeDtypeStruct((18 * SLOTS, MODES), jnp.bfloat16),
        in_specs=[smem, smem, vmem, vmem, vmem],
        out_specs=vmem,
        scratch_shapes=[pltpu.VMEM((72, SITES), jnp.float32)],
        compiler_params=pltpu.CompilerParams(vmem_limit_bytes=32 << 20),
        name="build_panel",
    )(sites, counts, modes, ahead, links)


def contract_kernel(panel_ref, table_ref, out_ref, side_ref, third_ref, hot_ref, pick_ref, cross_ref):
    total = FAR * ROWS
    lane = lax.broadcasted_iota(jnp.int32, (ROWS, MODES), 1)
    table = table_ref[...].astype(jnp.float32).T.astype(jnp.int32)
    for g in range(FAR):
        pair = table[0:ROWS, g : g + 1]
        first = (pair * 43691) >> 22
        second = pair - first * MODES
        hot_ref[0, g * ROWS : (g + 1) * ROWS, :] = jnp.where(lane == first, 1.0, 0.0)
        hot_ref[1, g * ROWS : (g + 1) * ROWS, :] = jnp.where(lane == second, 1.0, 0.0)

    wide = [panel_ref[d].astype(jnp.float32) for d in range(NEAR)]
    blank = jnp.zeros((KWIDE - NEAR * SLOTS, MODES), jnp.float32)

    def comp(k, c):
        at = (k * 6 + c) * SLOTS
        return jnp.concatenate([w[at : at + SLOTS] for w in wide] + [blank], axis=0)

    for k in range(2):
        for c in range(6):
            side_ref[k * 6 + c] = comp(k, c).astype(jnp.bfloat16)
    for k in range(3):
        t_re = comp(2, 2 * k)
        t_im = comp(2, 2 * k + 1)
        third_ref[2 * k * KWIDE : (2 * k + 1) * KWIDE, :] = jnp.concatenate(
            [t_re, t_im], axis=1
        ).astype(jnp.bfloat16)
        third_ref[(2 * k + 1) * KWIDE : (2 * k + 2) * KWIDE, :] = jnp.concatenate(
            [-t_im, t_re], axis=1
        ).astype(jnp.bfloat16)

    for k in range(2):
        hot = hot_ref[k].astype(jnp.bfloat16)

        @pl.loop(0, 6)
        def _(c):
            pick_ref[k * 6 + c] = lax.dot_general(
                hot, side_ref[k * 6 + c], (((1,), (1,)), ((), ())), preferred_element_type=jnp.float32
            )

    step = 16

    @pl.loop(0, total // step)
    def _(t):
        rows = pl.ds(pl.multiple_of(t * step, step), step)
        left = [pick_ref[c, rows, :] for c in range(6)]
        right = [pick_ref[6 + c, rows, :] for c in range(6)]

        def cmul(i, j):
            return (
                left[2 * i] * right[2 * j] - left[2 * i + 1] * right[2 * j + 1],
                left[2 * i] * right[2 * j + 1] + left[2 * i + 1] * right[2 * j],
            )

        for k, (i, j) in enumerate(((1, 2), (2, 0), (0, 1))):
            plus = cmul(i, j)
            minus = cmul(j, i)
            for r in range(2):
                at = (2 * k + r) * KWIDE
                cross_ref[rows, at : at + KWIDE] = (plus[r] - minus[r]).astype(jnp.bfloat16)

    summed = jnp.dot(cross_ref[...], third_ref[...], preferred_element_type=jnp.float32)
    half = lax.broadcasted_iota(jnp.int32, (40, LANES), 1) < 64
    for g in range(FAR):
        mine = summed[g * ROWS : (g + 1) * ROWS]
        tail = jnp.concatenate(
            [mine[:, LANES:], jnp.zeros((ROWS, 64), jnp.float32)], axis=1
        )
        lower = jnp.concatenate([tail[40:72], jnp.zeros((8, LANES), jnp.float32)], axis=0)
        packed = jnp.where(half, tail[0:40], pltpu.roll(lower, 64, 1))
        out_ref[g] = jnp.concatenate([mine[:, :LANES], packed], axis=0).astype(jnp.bfloat16)


def contract(panels, table):
    vmem = pl.BlockSpec(memory_space=pltpu.VMEM)
    total = FAR * ROWS
    return pl.pallas_call(
        contract_kernel,
        out_shape=jax.ShapeDtypeStruct((FAR, PACKED, LANES), jnp.bfloat16),
        in_specs=[vmem, vmem],
        out_specs=vmem,
        scratch_shapes=[
            pltpu.VMEM((12, KWIDE, MODES), jnp.bfloat16),
            pltpu.VMEM((6 * KWIDE, 2 * MODES), jnp.bfloat16),
            pltpu.VMEM((2, total, MODES), jnp.float32),
            pltpu.VMEM((12, total, KWIDE), jnp.float32),
            pltpu.VMEM((total, 6 * KWIDE), jnp.bfloat16),
        ],
        compiler_params=pltpu.CompilerParams(vmem_limit_bytes=48 << 20),
        name="contract_pairs",
    )(panels, table)


def total_kernel(scale, parts_ref, out_ref):
    total = parts_ref[0].astype(jnp.float32)
    for g in range(1, FAR):
        total = total + parts_ref[g].astype(jnp.float32)
    total = total * scale
    out_ref[:, 0:LANES] = total[0:ROWS]
    out_ref[0:40, LANES : 2 * MODES] = total[ROWS : ROWS + 40, 0:64]
    out_ref[40:72, LANES : 2 * MODES] = pltpu.roll(total[ROWS : ROWS + 32], 64, 1)[:, 0:64]


def add_up(parts):
    vmem = pl.BlockSpec(memory_space=pltpu.VMEM)
    scale = float(1.0 / (NEAR * FAR * SLOTS) ** 0.5)
    return pl.pallas_call(
        lambda *refs: total_kernel(scale, *refs),
        out_shape=jax.ShapeDtypeStruct((ROWS, 2 * MODES), jnp.float32),
        in_specs=[vmem],
        out_specs=vmem,
        name="add_up",
    )(parts)


def shards(modes, links, sites, counts, pair_table):
    count = lax.axis_size("gx")
    pairs = [(source, (source - 1) % count) for source in range(count)]
    ahead = lax.ppermute(modes[:, :, :PLANE], "gx", pairs)
    padded = jnp.pad(pair_table, (0, LANES - ROWS))
    tables = lax.all_to_all(
        jnp.broadcast_to(padded, (FAR, LANES)), "gx", 0, 0, axis_index_groups=FAR_GROUPS
    )
    panel = build(sites, counts, modes, ahead, links)
    panels = lax.all_gather(panel, "gx", axis_index_groups=NEAR_GROUPS)
    parts = contract(panels, tables)
    parts = lax.all_to_all(parts, "gx", 0, 0, axis_index_groups=FAR_GROUPS)
    return add_up(parts)


def solution(mesh):
    placed = (P("ta", None, "gx"), P("ta", None, "gx"), P(("ta", "gx")), P(("ta", "gx")), P("gx"))
    return jax.shard_map(
        shards, mesh=mesh, in_specs=placed, out_specs=P(("ta", "gx"), None), check_vma=False
    )
```

time: 259 us -> 70 us (0.27)
  the two profiles are of different devices: /device:TPU:2 before, /device:TPU:32 now
where the time goes in v1:
time: 70 us; the launch traced here: 69.7 us
  blocking collectives  38.4 us (55%)
  starting transfers between devices  13.6 us (19%)
  Pallas kernels  11.2 us (16%)
  local copies, waits for them, and re-layouts  5.84 us (8%)
    all_to_all x1, blocking collectives, shards(): parts = lax.all_to_all(parts, 'gx', 0, 0, axis_index_groups=FAR_GROUPS)  24.9 us
    all_gather x1, blocking collectives, shards(): panels = lax.all_gather(panel, 'gx', axis_index_groups=NEAR_GROUPS)  13.5 us
    all_to_all x1, starting transfers between devices, shards(): lax.all_to_all(jnp.broadcast_to(padded, (FAR, LANES)), 'gx', 0, 0, axis_i...  11.7 us
    pallas_call x1, Pallas kernels, contract(): pl.pallas_call(contract_kernel, out_shape=jax.ShapeDtypeStruct((FAR, PACK...  8.02 us
    unnamed x7, local copies, waits for them, and re-layouts  2.99 us
    ppermute x1, starting transfers between devices, shards(): ahead = lax.ppermute(modes[:, :, :PLANE], 'gx', pairs)  1.82 us
    pallas_call x1, Pallas kernels, add_up(): pl.pallas_call(lambda *refs: total_kernel(scale, *refs), out_shape=jax.Sh...  1.76 us
    pallas_call x1, Pallas kernels, build(): pl.pallas_call(build_kernel, out_shape=jax.ShapeDtypeStruct((18 * SLOTS,...  1.43 us
  transfers between devices with their start and end apart: 2, of which 0 were waited for; matrix products, arithmetic and copies ran while one was open for 3% of the time, Pallas kernels for 2%

profile of v1, /device:TPU:32, one launch (start us, length us, event | category | flops | bytes accessed | tf_op | source)
XLA Modules:
  0.0 69.7 jit_solution(7723464058563741001)
XLA Ops:
  0.0 1.0 %slice.3 = bf16[6,96,256]{2,1,0:T(8,128)(2,1)S(1)} slice(bf16[6,96,1024]{2,1,0:T(8,128)(2,1)} %modes_ref.1), slice={[0:6], [0:96], [0:256]} | slice | bytes 589824 | tf_op jit(solution)/shard_map/slice | solution.py:222
  1.0 1.8 %collective-permute-start = (bf16[6,96,256]{2,1,0:T(8,128)(2,1)S(1)}, bf16[6,96,256]{2,1,0:T(8,128)(2,1)S(1)}, u32[]{:S(2)}, u32[]{:S(2)}) collective-permute-start(bf16[6,96,256]{2,1,0:T(8,128)(2,1)S(1)} %slice.3), channel_id=1, source_target_pairs={{0,127},{1,0},{2,1},{3,2},{4,3},{5,4},{6,5},{7,6},{8,7},{9,8},{10,... | collective-permute-start | bytes 884744 | tf_op jit(solution)/shard_map/ppermute | solution.py:222
  2.8 0.7 pad.4
  3.5 0.6 broadcast_in_dim.3
  4.1 11.7 %all-to-all-start = ((s32[16,1,128]{2,1,0:T(1,128)}), s32[16,1,128]{2,1,0:T(1,128)S(1)}, u32[]{:S(2)}, u32[]{:S(2)}) async-start(s32[16,1,128]{2,1,0:T(1,128)} %broadcast_in_dim.3), calls=%async_computation | async-start | bytes 16384 | tf_op jit(solution)/shard_map/all_to_all | solution.py:224
  16.5 0.0 collective-permute-done.ahead_ref
  16.5 0.0 copy-start
  16.5 1.3 %copy-done = bf16[6,96,1024]{2,1,0:T(8,128)(2,1)S(1)} copy-done((bf16[6,96,1024]{2,1,0:T(8,128)(2,1)S(1)}, bf16[6,96,1024]{2,1,0:T(8,128)(2,1)}, u32[]{:S(2)}) %copy-start) | copy-done | bytes 1179672
  17.8 0.0 copy-start.1
  17.8 1.0 %copy-done.1 = f32[3,18,1024]{2,1,0:T(8,128)S(1)} copy-done((f32[3,18,1024]{2,1,0:T(8,128)S(1)}, f32[3,18,1024]{2,1,0:T(8,128)}, u32[]{:S(2)}) %copy-start.1) | copy-done | bytes 221208
  18.7 0.0 copy-start.2
  18.7 0.7 copy-done.2
  19.4 1.4 %build_panel.1 = bf16[432,96]{1,0:T(8,128)(2,1)S(1)} custom-call(s32[24]{0:T(128)S(1)} %copy-done.2, s32[1]{0:T(128)S(6)} %copy.8.counts_ref, bf16[6,96,1024]{2,1,0:T(8,128)(2,1)S(1)} %copy-done, bf16[6,96,256]{2,1,0:T(8,128)(2,1)S(1)} %collective-permute-done.ahead_ref, f32[3,18,1024]{2,1,0:T(8,128)S(1)} %copy-done.1), custom_call_target="tpu_custom_call" | custom-call | tf_op jit(solution)/shard_map/build_panel/pallas_call | solution.py:93
  20.8 0.1 copy.6
  20.9 13.5 %all-gather.1 = bf16[8,432,96]{1,2,0:T(8,128)(2,1)S(1)} all-gather(bf16[1,432,96]{1,2,0:T(8,128)(2,1)S(1)} %copy.6), channel_id=2, replica_groups={{0,1,2,3,4,5,6,7},{8,9,10,11,12,13,14,15},{16,17,18,19,20,21,22,23},{24..., dimensions={0}, use_global_device_ids=true | all-gather | bytes 746496 | tf_op jit(solution)/shard_map/all_gather | solution.py:228
  34.4 0.6 copy.7.panel_ref
  35.0 0.0 all-to-all-done
  35.0 8.0 %contract_pairs.1 = bf16[16,112,128]{2,1,0:T(8,128)(2,1)S(1)} custom-call(bf16[8,432,96]{2,1,0:T(8,128)(2,1)S(1)} %copy.7.panel_ref, s32[16,128]{1,0:T(8,128)S(1)} %bitcast.3), custom_call_target="tpu_custom_call" | custom-call | tf_op jit(solution)/shard_map/contract_pairs/pallas_call | solution.py:180
  43.0 24.9 %all_to_all.13.refs_0_ = bf16[16,112,128]{2,1,0:T(8,128)(2,1)} all-to-all(bf16[16,112,128]{2,1,0:T(8,128)(2,1)S(1)} %contract_pairs.1), channel_id=1, replica_groups={{0,8,16,24,32,40,48,56,64,72,80,88,96,104,112,120},{1,9,17,25,33,41,49,..., dimensions={0} | all-to-all | bytes 917504 | tf_op jit(solution)/shard_map/all_to_all | solution.py:230
  67.9 1.8 %add_up.1 = f32[72,192]{1,0:T(8,128)} custom-call(bf16[16,112,128]{2,1,0:T(8,128)(2,1)} %all_to_all.13.refs_0_), custom_call_target="tpu_custom_call" | custom-call | tf_op jit(solution)/shard_map/add_up/pallas_call | solution.py:210
Async XLA Ops:
  1.0 15.5 %collective-permute-start = (bf16[6,96,256]{2,1,0:T(8,128)(2,1)S(1)}, bf16[6,96,256]{2,1,0:T(8,128)(2,1)S(1)}, u32[]{:S(2)}, u32[]{:S(2)}) collective-permute-start(bf16[6,96,256]{2,1,0:T(8,128)(2,1)S(1)} %slice.3), channel_id=1, source_target_pairs={{0,127},{1,0},{2,1},{3,2},{4,3},{5,4},{6,5},{7,6},{8,7},{9,8},{10,... | collective-permute-start | bytes 884744 | tf_op jit(solution)/shard_map/ppermute | solution.py:222
  4.1 30.9 %all-to-all-start = ((s32[16,1,128]{2,1,0:T(1,128)}), s32[16,1,128]{2,1,0:T(1,128)S(1)}, u32[]{:S(2)}, u32[]{:S(2)}) async-start(s32[16,1,128]{2,1,0:T(1,128)} %broadcast_in_dim.3), calls=%async_computation | async-start | bytes 16384 | tf_op jit(solution)/shard_map/all_to_all | solution.py:224
  16.5 1.3 %copy-start = (bf16[6,96,1024]{2,1,0:T(8,128)(2,1)S(1)}, bf16[6,96,1024]{2,1,0:T(8,128)(2,1)}, u32[]{:S(2)}) copy-start(bf16[6,96,1024]{2,1,0:T(8,128)(2,1)} %modes_ref.1) | copy-start | bytes 3538948
  17.8 1.0 %copy-start.1 = (f32[3,18,1024]{2,1,0:T(8,128)S(1)}, f32[3,18,1024]{2,1,0:T(8,128)}, u32[]{:S(2)}) copy-start(f32[3,18,1024]{2,1,0:T(8,128)} %links_ref.1) | copy-start | bytes 663556
  18.7 0.7 copy-start.2

commit v2 on v1

v2 whole, which is shorter than its diff:
```python
import jax
import jax.numpy as jnp
from jax import lax
from jax.experimental import pallas as pl
from jax.experimental.pallas import tpu as pltpu
from jax.sharding import PartitionSpec as P

MODES = 96
LY = 16
LZ = 16
PLANE = LY * LZ
SITES = 1024
SLOTS = 24
ROWS = 72
NEAR = 8
FAR = 16
LANES = 128
KWIDE = 256
FAR_GROUPS = [[NEAR * j + i for j in range(FAR)] for i in range(NEAR)]
PACKED = 112
WIRE = 336


def local_kernel(
    sites_hbm, counts_ref, modes_hbm, links_hbm, vec_ref, link_ref, marks_ref,
    sites_ref, modes_ref, links_ref, rows_ref, sems,
):
    copies = [
        pltpu.make_async_copy(sites_hbm, sites_ref, sems.at[0]),
        pltpu.make_async_copy(links_hbm, links_ref, sems.at[1]),
    ] + [pltpu.make_async_copy(modes_hbm.at[c], modes_ref.at[c], sems.at[2 + c]) for c in range(6)]
    for copy in copies:
        copy.start()
    lane = lax.broadcasted_iota(jnp.int32, (1, LANES), 1)
    slot = jnp.where(lane < SLOTS, lane, jnp.where(lane < 2 * SLOTS, lane - SLOTS, lane - 2 * SLOTS))
    copies[0].wait()
    site = jnp.zeros((1, LANES), jnp.int32)
    for s in range(SLOTS):
        site = jnp.where(slot == s, sites_ref[s], site)
    z = site & (LZ - 1)
    y = (site >> 4) & (LY - 1)
    base = site - (y << 4) - z
    near = jnp.where(
        lane < SLOTS,
        site + PLANE,
        jnp.where(
            lane < 2 * SLOTS,
            base + (((y + 1) & (LY - 1)) << 4) + z,
            base + (y << 4) + ((z + 1) & (LZ - 1)),
        ),
    )
    used = lane < 3 * SLOTS
    near = jnp.where(used, near, -1)
    at = jnp.where(used, site, -1)
    marks_ref[0:1, :] = near - SITES
    marks_ref[1:2, :] = jnp.where(slot < counts_ref[0], 1, 0)
    row = lax.broadcasted_iota(jnp.int32, (SITES, LANES), 0)
    pick = jnp.where(row == near, 1.0, 0.0).astype(jnp.bfloat16)
    pick_site = jnp.where(row == at, 1.0, 0.0).astype(jnp.bfloat16)

    rows_ref[...] = jnp.zeros_like(rows_ref)
    copies[1].wait()
    for k in range(3):
        rows_ref[24 * k : 24 * k + 18, :] = links_ref[k]
    exact = rows_ref[...]
    high = exact.astype(jnp.bfloat16).astype(jnp.float32)
    rest = exact - high
    middle = rest.astype(jnp.bfloat16).astype(jnp.float32)
    low = rest - middle
    split = jnp.concatenate([high, middle, low], axis=0).astype(jnp.bfloat16)
    found = jnp.dot(split, pick_site, preferred_element_type=jnp.float32)
    found = found[0:72] + found[72:144] + found[144:216]
    link_ref[...] = jnp.where(
        lane < SLOTS, found[0:24], jnp.where(lane < 2 * SLOTS, found[24:48], found[48:72])
    )
    for c in range(6):
        copies[2 + c].wait()
    field = modes_ref[...].reshape(6 * MODES, SITES)
    vec_ref[...] = jnp.dot(field, pick, preferred_element_type=jnp.float32)


def pinned(value):
    return pltpu.with_memory_space_constraint(value, pltpu.HBM)


def build_local(sites, counts, modes, links):
    vmem = pl.BlockSpec(memory_space=pltpu.VMEM)
    hbm = pl.BlockSpec(memory_space=pltpu.HBM)
    return pl.pallas_call(
        local_kernel,
        out_shape=(
            pltpu.VMEM((6 * MODES, LANES), jnp.float32),
            pltpu.VMEM((24, LANES), jnp.float32),
            pltpu.VMEM((8, LANES), jnp.int32),
        ),
        in_specs=[hbm, pl.BlockSpec(memory_space=pltpu.SMEM), hbm, hbm],
        out_specs=(vmem, vmem, vmem),
        scratch_shapes=[
            pltpu.SMEM((SLOTS,), jnp.int32),
            pltpu.VMEM((6, MODES, SITES), jnp.bfloat16),
            pltpu.VMEM((3, 18, SITES), jnp.float32),
            pltpu.VMEM((72, SITES), jnp.float32),
            pltpu.SemaphoreType.DMA((8,)),
        ],
        compiler_params=pltpu.CompilerParams(vmem_limit_bytes=16 << 20),
        cost_estimate=pl.CostEstimate(flops=200_000_000, bytes_accessed=6_000_000, transcendentals=0),
        name="local_vectors",
    )(pinned(sites), counts, pinned(modes), pinned(links))


def build_kernel(vec_ref, link_ref, marks_ref, ahead_ref, out_ref):
    row = lax.broadcasted_iota(jnp.int32, (PLANE, LANES), 0)
    pick_ahead = jnp.where(row == marks_ref[0:1, :], 1.0, 0.0).astype(jnp.bfloat16)
    ahead = ahead_ref[...].reshape(6 * MODES, PLANE)
    vec = vec_ref[...] + jnp.dot(ahead, pick_ahead, preferred_element_type=jnp.float32)
    live = marks_ref[1:2, :] > 0
    link = link_ref[...]
    blank = jnp.zeros((LANES - MODES, LANES), jnp.float32)
    turned = []
    for i in range(3):
        real_part = jnp.zeros((MODES, LANES), jnp.float32)
        imag_part = jnp.zeros((MODES, LANES), jnp.float32)
        for j in range(3):
            at_ij = (i * 3 + j) * 2
            link_re = link[at_ij : at_ij + 1]
            link_im = link[at_ij + 1 : at_ij + 2]
            vec_re = vec[2 * j * MODES : (2 * j + 1) * MODES]
            vec_im = vec[(2 * j + 1) * MODES : (2 * j + 2) * MODES]
            real_part = real_part + link_re * vec_re - link_im * vec_im
            imag_part = imag_part + link_re * vec_im + link_im * vec_re
        for part in (real_part, imag_part):
            turned.append(jnp.concatenate([jnp.where(live, part, 0.0), blank], axis=0).T)
    panel = [turned[c][k * SLOTS : (k + 1) * SLOTS] for k in range(3) for c in range(6)]
    main = jnp.concatenate(panel[:14], axis=0)
    tail = jnp.concatenate(panel[14:], axis=0)
    spread = jnp.concatenate(
        [pltpu.roll(tail, 96, 1), pltpu.roll(tail, 64, 1), pltpu.roll(tail, 32, 1),
         jnp.zeros((WIRE - 288, LANES), jnp.float32)],
        axis=0,
    )
    lane = lax.broadcasted_iota(jnp.int32, (1, LANES), 1)
    out_ref[...] = jnp.where(lane < MODES, main, spread).astype(jnp.bfloat16)


def build(vec, link, marks, ahead):
    vmem = pl.BlockSpec(memory_space=pltpu.VMEM)
    return pl.pallas_call(
        build_kernel,
        out_shape=jax.ShapeDtypeStruct((WIRE, LANES), jnp.bfloat16),
        in_specs=[vmem] * 4,
        out_specs=vmem,
        compiler_params=pltpu.CompilerParams(vmem_limit_bytes=16 << 20),
        name="build_panel",
    )(vec, link, marks, ahead)


def contract_kernel(*refs):
    panel_refs, (table_ref, out_ref, side_ref, third_ref, pick_ref, cross_ref) = refs[:NEAR], refs[NEAR:]
    total = FAR * ROWS
    lane = lax.broadcasted_iota(jnp.int32, (1, LANES), 1)
    table = jnp.concatenate(
        [table_ref[...].astype(jnp.float32), jnp.zeros((FAR, LANES - ROWS), jnp.float32)], axis=1
    ).T.astype(jnp.int32)
    first_hot = []
    second_hot = []
    for g in range(FAR):
        pair = table[0:ROWS, g : g + 1]
        first = (pair * 43691) >> 22
        second = pair - first * MODES
        first_hot.append(jnp.where(lane == first, 1.0, 0.0))
        second_hot.append(jnp.where(lane == second, 1.0, 0.0))
    hots = [jnp.concatenate(h, axis=0).astype(jnp.bfloat16) for h in (first_hot, second_hot)]

    blank = jnp.zeros((KWIDE - NEAR * SLOTS, LANES), jnp.float32)
    comps = [[] for _ in range(18)]
    for ref in panel_refs:
        wide = ref[...].astype(jnp.float32)
        for n in range(14):
            comps[n].append(wide[n * SLOTS : (n + 1) * SLOTS])
        tail = jnp.where(
            lane < 32,
            pltpu.roll(wide[0:96], 32, 1),
            jnp.where(lane < 64, pltpu.roll(wide[96:192], 64, 1), pltpu.roll(wide[192:288], 96, 1)),
        )
        for n in range(4):
            comps[14 + n].append(tail[n * SLOTS : (n + 1) * SLOTS])
    for n in range(12):
        side_ref[n] = jnp.concatenate(comps[n] + [blank], axis=0).astype(jnp.bfloat16)
    for k in range(3):
        t_re = jnp.concatenate(comps[12 + 2 * k] + [blank], axis=0)
        t_im = jnp.concatenate(comps[13 + 2 * k] + [blank], axis=0)
        for r, (left, right) in enumerate(((t_re, t_im), (-t_im, t_re))):
            at = (2 * k + r) * KWIDE
            moved = pltpu.roll(right, 96, 1)
            third_ref[at : at + KWIDE, 0:LANES] = jnp.where(lane < 96, left, moved).astype(jnp.bfloat16)
            third_ref[at : at + KWIDE, LANES : 2 * LANES] = moved.astype(jnp.bfloat16)

    for k in range(2):
        hot = hots[k]

        @pl.loop(0, 6)
        def _(c):
            pick_ref[k * 6 + c] = lax.dot_general(
                hot, side_ref[k * 6 + c], (((1,), (1,)), ((), ())), preferred_element_type=jnp.float32
            )

    step = 16

    @pl.loop(0, total // step)
    def _(t):
        rows = pl.ds(pl.multiple_of(t * step, step), step)
        left = [pick_ref[c, rows, :] for c in range(6)]
        right = [pick_ref[6 + c, rows, :] for c in range(6)]

        def cmul(i, j):
            return (
                left[2 * i] * right[2 * j] - left[2 * i + 1] * right[2 * j + 1],
                left[2 * i] * right[2 * j + 1] + left[2 * i + 1] * right[2 * j],
            )

        for k, (i, j) in enumerate(((1, 2), (2, 0), (0, 1))):
            plus = cmul(i, j)
            minus = cmul(j, i)
            for r in range(2):
                at = (2 * k + r) * KWIDE
                cross_ref[rows, at : at + KWIDE] = (plus[r] - minus[r]).astype(jnp.bfloat16)

    half = lax.broadcasted_iota(jnp.int32, (40, LANES), 1) < 64
    summed = jnp.dot(cross_ref[...], third_ref[...], preferred_element_type=jnp.float32)
    for g in range(FAR):
        mine = summed[g * ROWS : (g + 1) * ROWS]
        tail = mine[:, LANES:]
        lower = jnp.concatenate([tail[40:72], jnp.zeros((8, LANES), jnp.float32)], axis=0)
        packed = jnp.where(half, tail[0:40], pltpu.roll(lower, 64, 1))
        out_ref[g] = jnp.concatenate([mine[:, :LANES], packed], axis=0).astype(jnp.bfloat16)


def contract(panels, table):
    vmem = pl.BlockSpec(memory_space=pltpu.VMEM)
    total = FAR * ROWS
    return pl.pallas_call(
        contract_kernel,
        out_shape=jax.ShapeDtypeStruct((FAR, PACKED, LANES), jnp.bfloat16),
        in_specs=[vmem] * (NEAR + 1),
        out_specs=vmem,
        scratch_shapes=[
            pltpu.VMEM((12, KWIDE, LANES), jnp.bfloat16),
            pltpu.VMEM((6 * KWIDE, 2 * LANES), jnp.bfloat16),
            pltpu.VMEM((12, total, KWIDE), jnp.float32),
            pltpu.VMEM((total, 6 * KWIDE), jnp.bfloat16),
        ],
        compiler_params=pltpu.CompilerParams(vmem_limit_bytes=48 << 20),
        name="contract_pairs",
    )(*panels, table)


def total_kernel(scale, parts_ref, out_ref):
    total = parts_ref[0].astype(jnp.float32)
    for g in range(1, FAR):
        total = total + parts_ref[g].astype(jnp.float32)
    total = total * scale
    out_ref[:, 0:LANES] = total[0:ROWS]
    out_ref[0:40, LANES : 2 * MODES] = total[ROWS : ROWS + 40, 0:64]
    out_ref[40:72, LANES : 2 * MODES] = pltpu.roll(total[ROWS : ROWS + 32], 64, 1)[:, 0:64]


def add_up(parts):
    vmem = pl.BlockSpec(memory_space=pltpu.VMEM)
    scale = float(1.0 / (NEAR * FAR * SLOTS) ** 0.5)
    return pl.pallas_call(
        lambda *refs: total_kernel(scale, *refs),
        out_shape=jax.ShapeDtypeStruct((ROWS, 2 * MODES), jnp.float32),
        in_specs=[vmem],
        out_specs=vmem,
        compiler_params=pltpu.CompilerParams(vmem_limit_bytes=8 << 20),
        name="add_up",
    )(parts)


def swapped(value, bits):
    count = lax.axis_size("gx")
    return lax.ppermute(value, "gx", [(source, source ^ bits) for source in range(count)])


def shards(modes, links, sites, counts, pair_table):
    count = lax.axis_size("gx")
    pairs = [(source, (source - 1) % count) for source in range(count)]
    ahead = lax.ppermute(modes[:, :, :PLANE], "gx", pairs)
    tables = lax.all_to_all(
        jnp.broadcast_to(pair_table, (FAR, ROWS)), "gx", 0, 0, axis_index_groups=FAR_GROUPS
    )
    vec, link, marks = build_local(sites, counts, modes, links)
    panel = build(vec, link, marks, ahead)
    panel, tables = lax.optimization_barrier((panel, tables))
    others = [swapped(panel, bits) for bits in (2, 4, 6)]
    panels = [panel] + others
    panels = panels + [swapped(p, 1) for p in panels]
    parts = contract(panels, tables)
    parts = lax.all_to_all(parts, "gx", 0, 0, axis_index_groups=FAR_GROUPS)
    return add_up(parts)


def solution(mesh):
    placed = (P("ta", None, "gx"), P("ta", None, "gx"), P(("ta", "gx")), P(("ta", "gx")), P("gx"))
    return jax.shard_map(
        shards, mesh=mesh, in_specs=placed, out_specs=P(("ta", "gx"), None), check_vma=False
    )
```

time: 70 us -> 62 us (0.89)
  the two profiles are of different devices: /device:TPU:32 before, /device:TPU:2 now
where the time goes in v2:
time: 62 us; the launch traced here: 61.8 us
  blocking collectives  18.9 us (30%)
  starting transfers between devices  16.3 us (26%)
  waiting for transfers between devices  12.5 us (20%)
  Pallas kernels  11.2 us (18%)
  local copies, waits for them, and re-layouts  2.24 us (4%)
  between operations  0.71 us (1%)
    all_to_all x1, blocking collectives, shards(): parts = lax.all_to_all(parts, 'gx', 0, 0, axis_index_groups=FAR_GROUPS)  18.9 us
    all_to_all x1, starting transfers between devices, shards(): lax.all_to_all(jnp.broadcast_to(pair_table, (FAR, ROWS)), 'gx', 0, 0, axi...  11.2 us
    pallas_call x1, Pallas kernels, contract(): pl.pallas_call(contract_kernel, out_shape=jax.ShapeDtypeStruct((FAR, PACK...  8.05 us
    all_to_all x1, waiting for transfers between devices, shards(): lax.all_to_all(jnp.broadcast_to(pair_table, (FAR, ROWS)), 'gx', 0, 0, axi...  6.82 us
    ppermute x7, waiting for transfers between devices, swapped(): lax.ppermute(value, 'gx', [(source, source ^ bits) for source in range(co...  5.7 us
    ppermute x7, starting transfers between devices, swapped(): lax.ppermute(value, 'gx', [(source, source ^ bits) for source in range(co...  4.99 us
    pallas_call x1, Pallas kernels, build_local(): pl.pallas_call(local_kernel, out_shape=(pltpu.VMEM((6 * MODES, LANES), jn...  1.92 us
    broadcast_in_dim x1, local copies, waits for them, and re-layouts, shards(): jnp.broadcast_to(pair_table, (FAR, ROWS))  1.26 us
  transfers between devices with their start and end apart: 9, of which 5 were waited for; matrix products, arithmetic and copies ran while one was open for 2% of the time, Pallas kernels for 4%

profile of v2, /device:TPU:2, one launch (start us, length us, event | category | flops | bytes accessed | tf_op | source)
XLA Modules:
  0.0 61.8 jit_solution(13753322943725297877)
XLA Ops:
  0.0 1.0 %slice.3 = bf16[6,96,256]{2,1,0:T(8,128)(2,1)S(1)} slice(bf16[6,96,1024]{2,1,0:T(8,128)(2,1)} %modes_hbm.1), slice={[0:6], [0:96], [0:256]} | slice | bytes 589824 | tf_op jit(solution)/shard_map/slice | solution.py:288
  1.0 0.1 collective-permute-start
  1.1 1.3 %broadcast_in_dim.3 = s32[16,1,72]{2,1,0:T(1,128)} broadcast(s32[72]{0:T(128)} %param.9), dimensions={2} | broadcast | bytes 4896 | tf_op jit(solution)/shard_map/broadcast_in_dim | solution.py:290
  2.3 11.2 %all-to-all-start = ((s32[16,1,72]{2,1,0:T(1,128)}), s32[16,1,72]{2,1,0:T(1,128)S(1)}, u32[]{:S(2)}, u32[]{:S(2)}) async-start(s32[16,1,72]{2,1,0:T(1,128)} %broadcast_in_dim.3), calls=%async_computation | async-start | bytes 16384 | tf_op jit(solution)/shard_map/all_to_all | solution.py:289
  14.2 1.9 %local_vectors.1 = (f32[576,128]{1,0:T(8,128)S(1)}, f32[24,128]{1,0:T(8,128)S(1)}, s32[8,128]{1,0:T(8,128)S(1)}) custom-call(s32[24]{0:T(128)} %sites_hbm.1, s32[1]{0:T(128)S(6)} %copy.6.counts_ref, bf16[6,96,1024]{2,1,0:T(8,128)(2,1)} %modes_hbm.1, f32[3,18,1024]{2,1,0:T(8,128)} %links_hbm.1), custom_call_target="tpu_custom_call" | custom-call | flops 200000000 | bytes 6000000 | tf_op jit(solution)/shard_map/local_vectors/pallas_call | solution.py:89
  16.1 0.0 collective-permute-done.ahead_ref
  16.1 0.5 build_panel.1.refs_0_
  16.6 6.8 %all-to-all-done = s32[16,1,72]{2,1,0:T(1,128)S(1)} async-done(((s32[16,1,72]{2,1,0:T(1,128)}), s32[16,1,72]{2,1,0:T(1,128)S(1)}, u32[]{:S(2)}, u32[]{:S(2)}) %all-to-all-start) | async-done | bytes 4640 | tf_op jit(solution)/shard_map/all_to_all | solution.py:289
  23.4 1.5 %collective-permute-start.3 = (bf16[336,128]{1,0:T(8,128)(2,1)S(1)}, bf16[336,128]{1,0:T(8,128)(2,1)S(1)}, u32[]{:S(2)}, u32[]{:S(2)}) collective-permute-start(bf16[336,128]{1,0:T(8,128)(2,1)S(1)} %build_panel.1.refs_0_), channel_id=1, source_target_pairs={{0,6},{1,7},{2,4},{3,5},{4,2},{5,3},{6,0},{7,1},{8,14},{9,15},{10,... | collective-permute-start | bytes 258056 | tf_op jit(solution)/shard_map/ppermute | solution.py:282
  24.9 3.4 %collective-permute-start.2 = (bf16[336,128]{1,0:T(8,128)(2,1)S(1)}, bf16[336,128]{1,0:T(8,128)(2,1)S(1)}, u32[]{:S(2)}, u32[]{:S(2)}) collective-permute-start(bf16[336,128]{1,0:T(8,128)(2,1)S(1)} %build_panel.1.refs_0_), channel_id=1, source_target_pairs={{0,4},{1,5},{2,6},{3,7},{4,0},{5,1},{6,2},{7,3},{8,12},{9,13},{10,... | collective-permute-start | bytes 258056 | tf_op jit(solution)/shard_map/ppermute | solution.py:282
  28.4 0.0 collective-permute-start.1
  28.4 0.0 collective-permute-start.4
  28.4 0.5 collective-permute-done.3.refs_3_
  28.8 0.0 collective-permute-start.7
  28.9 2.0 %collective-permute-done.2.refs_2_ = bf16[336,128]{1,0:T(8,128)(2,1)S(1)} collective-permute-done((bf16[336,128]{1,0:T(8,128)(2,1)S(1)}, bf16[336,128]{1,0:T(8,128)(2,1)S(1)}, u32[]{:S(2)}, u32[]{:S(2)}) %collective-permute-start.2) | collective-permute-done | bytes 86048 | tf_op jit(solution)/shard_map/ppermute | solution.py:282
  30.9 0.0 collective-permute-start.6
  30.9 1.9 %collective-permute-done.1.refs_1_ = bf16[336,128]{1,0:T(8,128)(2,1)S(1)} collective-permute-done((bf16[336,128]{1,0:T(8,128)(2,1)S(1)}, bf16[336,128]{1,0:T(8,128)(2,1)S(1)}, u32[]{:S(2)}, u32[]{:S(2)}) %collective-permute-start.1) | collective-permute-done | bytes 86048 | tf_op jit(solution)/shard_map/ppermute | solution.py:282
  32.8 0.0 collective-permute-start.5
  32.9 0.0 collective-permute-done.4.refs_4_
  32.9 0.0 collective-permute-done.7.refs_7_
  32.9 0.0 collective-permute-done.6.refs_6_
  32.9 1.3 %collective-permute-done.5.refs_5_ = bf16[336,128]{1,0:T(8,128)(2,1)S(1)} collective-permute-done((bf16[336,128]{1,0:T(8,128)(2,1)S(1)}, bf16[336,128]{1,0:T(8,128)(2,1)S(1)}, u32[]{:S(2)}, u32[]{:S(2)}) %collective-permute-start.5) | collective-permute-done | bytes 86048 | tf_op jit(solution)/shard_map/ppermute | solution.py:282
  34.1 8.0 %contract_pairs.1 = bf16[16,112,128]{2,1,0:T(8,128)(2,1)S(1)} custom-call(bf16[336,128]{1,0:T(8,128)(2,1)S(1)} %build_panel.1.refs_0_, bf16[336,128]{1,0:T(8,128)(2,1)S(1)} %collective-permute-done.1.refs_1_, bf16[336,128]{1,0:T(8,128)(2,1)S(1)} %collective-permute-done.2.refs_2_, bf16[336,128]{1,0:T(8,128)(2,1)S(1)} %collective-permute-done.3.refs_3_, ...), custom_call_target="tpu_custom_call" | custom-call | tf_op jit(solution)/shard_map/contract_pairs/pallas_call | solution.py:241
  42.2 18.9 %all_to_all.14.refs_0_ = bf16[16,112,128]{2,1,0:T(8,128)(2,1)S(1)} all-to-all(bf16[16,112,128]{2,1,0:T(8,128)(2,1)S(1)} %contract_pairs.1), channel_id=1, replica_groups={{0,8,16,24,32,40,48,56,64,72,80,88,96,104,112,120},{1,9,17,25,33,41,49,..., dimensions={0} | all-to-all | bytes 917504 | tf_op jit(solution)/shard_map/all_to_all | solution.py:299
  61.0 0.7 %add_up.1 = f32[72,192]{1,0:T(8,128)} custom-call(bf16[16,112,128]{2,1,0:T(8,128)(2,1)S(1)} %all_to_all.14.refs_0_), custom_call_target="tpu_custom_call" | custom-call | tf_op jit(solution)/shard_map/add_up/pallas_call | solution.py:270
Async XLA Ops:
  1.0 15.1 %collective-permute-start = (bf16[6,96,256]{2,1,0:T(8,128)(2,1)S(1)}, bf16[6,96,256]{2,1,0:T(8,128)(2,1)S(1)}, u32[]{:S(2)}, u32[]{:S(2)}) collective-permute-start(bf16[6,96,256]{2,1,0:T(8,128)(2,1)S(1)} %slice.3), channel_id=1, source_target_pairs={{0,127},{1,0},{2,1},{3,2},{4,3},{5,4},{6,5},{7,6},{8,7},{9,8},{10,... | collective-permute-start | bytes 884744 | tf_op jit(solution)/shard_map/ppermute | solution.py:288
  2.3 21.1 %all-to-all-start = ((s32[16,1,72]{2,1,0:T(1,128)}), s32[16,1,72]{2,1,0:T(1,128)S(1)}, u32[]{:S(2)}, u32[]{:S(2)}) async-start(s32[16,1,72]{2,1,0:T(1,128)} %broadcast_in_dim.3), calls=%async_computation | async-start | bytes 16384 | tf_op jit(solution)/shard_map/all_to_all | solution.py:289
  23.4 5.4 %collective-permute-start.3 = (bf16[336,128]{1,0:T(8,128)(2,1)S(1)}, bf16[336,128]{1,0:T(8,128)(2,1)S(1)}, u32[]{:S(2)}, u32[]{:S(2)}) collective-permute-start(bf16[336,128]{1,0:T(8,128)(2,1)S(1)} %build_panel.1.refs_0_), channel_id=1, source_target_pairs={{0,6},{1,7},{2,4},{3,5},{4,2},{5,3},{6,0},{7,1},{8,14},{9,15},{10,... | collective-permute-start | bytes 258056 | tf_op jit(solution)/shard_map/ppermute | solution.py:282
  24.9 6.0 %collective-permute-start.2 = (bf16[336,128]{1,0:T(8,128)(2,1)S(1)}, bf16[336,128]{1,0:T(8,128)(2,1)S(1)}, u32[]{:S(2)}, u32[]{:S(2)}) collective-permute-start(bf16[336,128]{1,0:T(8,128)(2,1)S(1)} %build_panel.1.refs_0_), channel_id=1, source_target_pairs={{0,4},{1,5},{2,6},{3,7},{4,0},{5,1},{6,2},{7,3},{8,12},{9,13},{10,... | collective-permute-start | bytes 258056 | tf_op jit(solution)/shard_map/ppermute | solution.py:282
  28.4 4.5 %collective-permute-start.1 = (bf16[336,128]{1,0:T(8,128)(2,1)S(1)}, bf16[336,128]{1,0:T(8,128)(2,1)S(1)}, u32[]{:S(2)}, u32[]{:S(2)}) collective-permute-start(bf16[336,128]{1,0:T(8,128)(2,1)S(1)} %build_panel.1.refs_0_), channel_id=1, source_target_pairs={{0,2},{1,3},{2,0},{3,1},{4,6},{5,7},{6,4},{7,5},{8,10},{9,11},{10,... | collective-permute-start | bytes 258056 | tf_op jit(solution)/shard_map/ppermute | solution.py:282
  28.4 4.5 %collective-permute-start.4 = (bf16[336,128]{1,0:T(8,128)(2,1)S(1)}, bf16[336,128]{1,0:T(8,128)(2,1)S(1)}, u32[]{:S(2)}, u32[]{:S(2)}) collective-permute-start(bf16[336,128]{1,0:T(8,128)(2,1)S(1)} %build_panel.1.refs_0_), channel_id=1, source_target_pairs={{0,1},{1,0},{2,3},{3,2},{4,5},{5,4},{6,7},{7,6},{8,9},{9,8},{10,11... | collective-permute-start | bytes 258056 | tf_op jit(solution)/shard_map/ppermute | solution.py:282
  28.8 4.0 %collective-permute-start.7 = (bf16[336,128]{1,0:T(8,128)(2,1)S(1)}, bf16[336,128]{1,0:T(8,128)(2,1)S(1)}, u32[]{:S(2)}, u32[]{:S(2)}) collective-permute-start(bf16[336,128]{1,0:T(8,128)(2,1)S(1)} %collective-permute-done.3.refs_3_), channel_id=1, source_target_pairs={{0,1},{1,0},{2,3},{3,2},{4,5},{5,4},{6,7},{7,6},{8,9},{9,8},{10,11... | collective-permute-start | bytes 258056 | tf_op jit(solution)/shard_map/ppermute | solution.py:282
  30.9 2.0 %collective-permute-start.6 = (bf16[336,128]{1,0:T(8,128)(2,1)S(1)}, bf16[336,128]{1,0:T(8,128)(2,1)S(1)}, u32[]{:S(2)}, u32[]{:S(2)}) collective-permute-start(bf16[336,128]{1,0:T(8,128)(2,1)S(1)} %collective-permute-done.2.refs_2_), channel_id=1, source_target_pairs={{0,1},{1,0},{2,3},{3,2},{4,5},{5,4},{6,7},{7,6},{8,9},{9,8},{10,11... | collective-permute-start | bytes 258056 | tf_op jit(solution)/shard_map/ppermute | solution.py:282
  32.8 1.3 %collective-permute-start.5 = (bf16[336,128]{1,0:T(8,128)(2,1)S(1)}, bf16[336,128]{1,0:T(8,128)(2,1)S(1)}, u32[]{:S(2)}, u32[]{:S(2)}) collective-permute-start(bf16[336,128]{1,0:T(8,128)(2,1)S(1)} %collective-permute-done.1.refs_1_), channel_id=1, source_target_pairs={{0,1},{1,0},{2,3},{3,2},{4,5},{5,4},{6,7},{7,6},{8,9},{9,8},{10,11... | collective-permute-start | bytes 258056 | tf_op jit(solution)/shard_map/ppermute | solution.py:282

commit v3 on v2

--- a/solution.py
+++ b/solution.py
@@ -15,10 +15,41 @@
 NEAR = 8
 FAR = 16
 LANES = 128
-KWIDE = 256
 FAR_GROUPS = [[NEAR * j + i for j in range(FAR)] for i in range(NEAR)]
 PACKED = 112
 WIRE = 336
+
+
+def pinned(value):
+    return pltpu.with_memory_space_constraint(value, pltpu.HBM)
+
+
+def prepare_kernel(table_hbm, modes_hbm, plane_ref, tables_ref, table_ref, sems):
+    small = pltpu.make_async_copy(table_hbm, table_ref, sems.at[0])
+    small.start()
+    copy = pltpu.make_async_copy(modes_hbm.at[:, :, pl.ds(0, PLANE)], plane_ref, sems.at[1])
+    copy.start()
+    small.wait()
+    row = jnp.concatenate([table_ref[...], jnp.zeros((1, LANES - ROWS), jnp.int32)], axis=1)
+    for g in range(FAR):
+        tables_ref[g] = jnp.broadcast_to(row, (16, LANES))
+    copy.wait()
+
+
+def prepare(modes, pair_table):
+    vmem = pl.BlockSpec(memory_space=pltpu.VMEM)
+    return pl.pallas_call(
+        prepare_kernel,
+        out_shape=(
+            pltpu.VMEM((6, MODES, PLANE), jnp.bfloat16),
+            pltpu.VMEM((FAR, 16, LANES), jnp.int32),
+        ),
+        in_specs=[pl.BlockSpec(memory_space=pltpu.HBM)] * 2,
+        out_specs=(vmem, vmem),
+        scratch_shapes=[pltpu.VMEM((1, ROWS), jnp.int32), pltpu.SemaphoreType.DMA((2,))],
+        compiler_params=pltpu.CompilerParams(vmem_limit_bytes=8 << 20),
+        name="prepare",
+    )(pinned(pair_table.reshape(1, ROWS)), pinned(modes))
 
 
 def local_kernel(
@@ -79,10 +110,6 @@
     vec_ref[...] = jnp.dot(field, pick, preferred_element_type=jnp.float32)
 
 
-def pinned(value):
-    return pltpu.with_memory_space_constraint(value, pltpu.HBM)
-
-
 def build_local(sites, counts, modes, links):
     vmem = pl.BlockSpec(memory_space=pltpu.VMEM)
     hbm = pl.BlockSpec(memory_space=pltpu.HBM)
@@ -154,24 +181,29 @@
     )(vec, link, marks, ahead)
 
 
+TILES = ((0, 256), (256, 256), (512, 256), (768, 256), (1024, 128))
+SHARED = NEAR * SLOTS
+STACK = 6 * SHARED
+
+
 def contract_kernel(*refs):
-    panel_refs, (table_ref, out_ref, side_ref, third_ref, pick_ref, cross_ref) = refs[:NEAR], refs[NEAR:]
-    total = FAR * ROWS
+    panel_refs = refs[:NEAR]
+    table_ref, out_ref, side_ref, third_ref, *scratch = refs[NEAR:]
+    pick_refs, cross_refs = scratch[:4], scratch[4:]
     lane = lax.broadcasted_iota(jnp.int32, (1, LANES), 1)
-    table = jnp.concatenate(
-        [table_ref[...].astype(jnp.float32), jnp.zeros((FAR, LANES - ROWS), jnp.float32)], axis=1
-    ).T.astype(jnp.int32)
-    first_hot = []
-    second_hot = []
+
+    rows = [table_ref[g][0:1] for g in range(FAR)]
+    pieces = [
+        jnp.where(lane < 64, rows[2 * v], pltpu.roll(rows[2 * v + 1], 64, 1)) for v in range(FAR // 2)
+    ]
+    last = jnp.zeros((1, LANES), jnp.int32)
     for g in range(FAR):
-        pair = table[0:ROWS, g : g + 1]
-        first = (pair * 43691) >> 22
-        second = pair - first * MODES
-        first_hot.append(jnp.where(lane == first, 1.0, 0.0))
-        second_hot.append(jnp.where(lane == second, 1.0, 0.0))
-    hots = [jnp.concatenate(h, axis=0).astype(jnp.bfloat16) for h in (first_hot, second_hot)]
-
-    blank = jnp.zeros((KWIDE - NEAR * SLOTS, LANES), jnp.float32)
+        moved = pltpu.roll(rows[g], (8 * g - 64) % LANES, 1) if g != 8 else rows[g]
+        last = jnp.where((lane >= 8 * g) & (lane < 8 * g + 8), moved, last)
+    pairs = jnp.concatenate(pieces + [last], axis=1)
+    first = (pairs * 43691) >> 22
+    second = pairs - first * MODES
+
     comps = [[] for _ in range(18)]
     for ref in panel_refs:
         wide = ref[...].astype(jnp.float32)
@@ -184,74 +216,102 @@
         )
         for n in range(4):
             comps[14 + n].append(tail[n * SLOTS : (n + 1) * SLOTS])
+    comps = [jnp.concatenate(c, axis=0) for c in comps]
     for n in range(12):
-        side_ref[n] = jnp.concatenate(comps[n] + [blank], axis=0).astype(jnp.bfloat16)
-    for k in range(3):
-        t_re = jnp.concatenate(comps[12 + 2 * k] + [blank], axis=0)
-        t_im = jnp.concatenate(comps[13 + 2 * k] + [blank], axis=0)
-        for r, (left, right) in enumerate(((t_re, t_im), (-t_im, t_re))):
-            at = (2 * k + r) * KWIDE
-            moved = pltpu.roll(right, 96, 1)
-            third_ref[at : at + KWIDE, 0:LANES] = jnp.where(lane < 96, left, moved).astype(jnp.bfloat16)
-            third_ref[at : at + KWIDE, LANES : 2 * LANES] = moved.astype(jnp.bfloat16)
-
-    for k in range(2):
-        hot = hots[k]
-
-        @pl.loop(0, 6)
-        def _(c):
-            pick_ref[k * 6 + c] = lax.dot_general(
-                hot, side_ref[k * 6 + c], (((1,), (1,)), ((), ())), preferred_element_type=jnp.float32
+        side_ref[n // 6, (n % 6) * SHARED : (n % 6 + 1) * SHARED, :] = comps[n].astype(jnp.bfloat16)
+
+    def third():
+        upper = []
+        lower = []
+        for k in range(3):
+            t_re, t_im = comps[12 + 2 * k], comps[13 + 2 * k]
+            upper += [t_re, -t_im]
+            lower += [t_im, t_re]
+        third_ref[0:MODES, :] = jnp.concatenate(upper, axis=0).T[0:MODES].astype(jnp.bfloat16)
+        third_ref[MODES : 2 * MODES, :] = jnp.concatenate(lower, axis=0).T[0:MODES].astype(jnp.bfloat16)
+
+    half = lane < 64
+
+    def select(t):
+        at, width = TILES[t]
+        mode = lax.broadcasted_iota(jnp.int32, (LANES, width), 0)
+        for n, index in enumerate((first, second)):
+            hot = jnp.where(mode == index[:, at : at + width], 1.0, 0.0).astype(jnp.bfloat16)
+            pick_refs[2 * (t % 2) + n][:, 0:width] = jnp.dot(
+                side_ref[n], hot, preferred_element_type=jnp.float32
             )
 
-    step = 16
-
-    @pl.loop(0, total // step)
-    def _(t):
-        rows = pl.ds(pl.multiple_of(t * step, step), step)
-        left = [pick_ref[c, rows, :] for c in range(6)]
-        right = [pick_ref[6 + c, rows, :] for c in range(6)]
-
-        def cmul(i, j):
-            return (
-                left[2 * i] * right[2 * j] - left[2 * i + 1] * right[2 * j + 1],
-                left[2 * i] * right[2 * j + 1] + left[2 * i + 1] * right[2 * j],
+    def cross(t):
+        at, width = TILES[t]
+        lefts, rights, target = pick_refs[2 * (t % 2)], pick_refs[2 * (t % 2) + 1], cross_refs[t % 2]
+
+        def chunk(q):
+            left = [lefts[pl.ds(c * SHARED + q, 16), 0:width] for c in range(6)]
+            right = [rights[pl.ds(c * SHARED + q, 16), 0:width] for c in range(6)]
+
+            def cmul(i, j):
+                return (
+                    left[2 * i] * right[2 * j] - left[2 * i + 1] * right[2 * j + 1],
+                    left[2 * i] * right[2 * j + 1] + left[2 * i + 1] * right[2 * j],
+                )
+
+            for k, (i, j) in enumerate(((1, 2), (2, 0), (0, 1))):
+                plus = cmul(i, j)
+                minus = cmul(j, i)
+                for r in range(2):
+                    target[pl.ds((2 * k + r) * SHARED + q, 16), 0:width] = (plus[r] - minus[r]).astype(
+                        jnp.bfloat16
+                    )
+
+        for q in range(0, SHARED, 16):
+            chunk(q)
+
+    def finish(t):
+        at, width = TILES[t]
+        summed = jnp.dot(
+            third_ref[...], cross_refs[t % 2][:, 0:width], preferred_element_type=jnp.float32
+        )
+        if width == LANES:
+            flat = jnp.concatenate([summed, jnp.zeros((64, LANES), jnp.float32)], axis=0)
+            low, high = flat[0:LANES].T, flat[LANES : 2 * LANES].T
+            for g in range(FAR):
+                both = [low[8 * g : 8 * g + 8], high[8 * g : 8 * g + 8]]
+                out_ref[g, MODES : MODES + 16, :] = jnp.concatenate(both, axis=0).astype(jnp.bfloat16)
+            return
+        for v in range(2):
+            real = summed[0:MODES, v * LANES : (v + 1) * LANES]
+            imag = summed[MODES : 2 * MODES, v * LANES : (v + 1) * LANES]
+            g = at // 64 + 2 * v
+            out_ref[g, 0:MODES, :] = jnp.where(half, real, pltpu.roll(imag, 64, 1)).astype(jnp.bfloat16)
+            out_ref[g + 1, 0:MODES, :] = jnp.where(half, pltpu.roll(real, 64, 1), imag).astype(
+                jnp.bfloat16
             )
 
-        for k, (i, j) in enumerate(((1, 2), (2, 0), (0, 1))):
-            plus = cmul(i, j)
-            minus = cmul(j, i)
-            for r in range(2):
-                at = (2 * k + r) * KWIDE
-                cross_ref[rows, at : at + KWIDE] = (plus[r] - minus[r]).astype(jnp.bfloat16)
-
-    half = lax.broadcasted_iota(jnp.int32, (40, LANES), 1) < 64
-    summed = jnp.dot(cross_ref[...], third_ref[...], preferred_element_type=jnp.float32)
-    for g in range(FAR):
-        mine = summed[g * ROWS : (g + 1) * ROWS]
-        tail = mine[:, LANES:]
-        lower = jnp.concatenate([tail[40:72], jnp.zeros((8, LANES), jnp.float32)], axis=0)
-        packed = jnp.where(half, tail[0:40], pltpu.roll(lower, 64, 1))
-        out_ref[g] = jnp.concatenate([mine[:, :LANES], packed], axis=0).astype(jnp.bfloat16)
-
-
-def contract(panels, table):
-    vmem = pl.BlockSpec(memory_space=pltpu.VMEM)
-    total = FAR * ROWS
+    select(0)
+    third()
+    for t in range(len(TILES)):
+        if t + 1 < len(TILES):
+            select(t + 1)
+        cross(t)
+        finish(t)
+
+
+def contract(panels, tables):
+    vmem = pl.BlockSpec(memory_space=pltpu.VMEM)
     return pl.pallas_call(
         contract_kernel,
         out_shape=jax.ShapeDtypeStruct((FAR, PACKED, LANES), jnp.bfloat16),
         in_specs=[vmem] * (NEAR + 1),
         out_specs=vmem,
         scratch_shapes=[
-            pltpu.VMEM((12, KWIDE, LANES), jnp.bfloat16),
-            pltpu.VMEM((6 * KWIDE, 2 * LANES), jnp.bfloat16),
-            pltpu.VMEM((12, total, KWIDE), jnp.float32),
-            pltpu.VMEM((total, 6 * KWIDE), jnp.bfloat16),
-        ],
-        compiler_params=pltpu.CompilerParams(vmem_limit_bytes=48 << 20),
+            pltpu.VMEM((2, STACK, LANES), jnp.bfloat16),
+            pltpu.VMEM((2 * MODES, STACK), jnp.bfloat16),
+        ]
+        + [pltpu.VMEM((STACK, 256), jnp.float32)] * 4
+        + [pltpu.VMEM((STACK, 256), jnp.bfloat16)] * 2,
+        compiler_params=pltpu.CompilerParams(vmem_limit_bytes=40 << 20),
         name="contract_pairs",
-    )(*panels, table)
+    )(*panels, tables)
 
 
 def total_kernel(scale, parts_ref, out_ref):
@@ -259,9 +319,13 @@
     for g in range(1, FAR):
         total = total + parts_ref[g].astype(jnp.float32)
     total = total * scale
-    out_ref[:, 0:LANES] = total[0:ROWS]
-    out_ref[0:40, LANES : 2 * MODES] = total[ROWS : ROWS + 40, 0:64]
-    out_ref[40:72, LANES : 2 * MODES] = pltpu.roll(total[ROWS : ROWS + 32], 64, 1)[:, 0:64]
+    lane = lax.broadcasted_iota(jnp.int32, (1, LANES), 1)
+    main = jnp.concatenate([total[0:MODES], jnp.zeros((LANES - MODES, LANES), jnp.float32)], axis=0).T
+    moved = pltpu.roll(main[64:128], 96, 1)
+    out_ref[0:64, 0:LANES] = jnp.where(lane < MODES, main[0:64], moved)
+    out_ref[0:64, LANES : 2 * MODES] = moved[:, 0:64]
+    out_ref[64:72, 0:LANES] = total[MODES : MODES + 8]
+    out_ref[64:72, LANES : 2 * MODES] = total[MODES + 8 : MODES + 16, 0:64]
 
 
 def add_up(parts):
@@ -285,13 +349,11 @@
 def shards(modes, links, sites, counts, pair_table):
     count = lax.axis_size("gx")
     pairs = [(source, (source - 1) % count) for source in range(count)]
-    ahead = lax.ppermute(modes[:, :, :PLANE], "gx", pairs)
-    tables = lax.all_to_all(
-        jnp.broadcast_to(pair_table, (FAR, ROWS)), "gx", 0, 0, axis_index_groups=FAR_GROUPS
-    )
+    plane, tables = prepare(modes, pair_table)
+    ahead = lax.ppermute(plane, "gx", pairs)
+    tables = lax.all_to_all(tables, "gx", 0, 0, axis_index_groups=FAR_GROUPS)
     vec, link, marks = build_local(sites, counts, modes, links)
     panel = build(vec, link, marks, ahead)
-    panel, tables = lax.optimization_barrier((panel, tables))
     others = [swapped(panel, bits) for bits in (2, 4, 6)]
     panels = [panel] + others
     panels = panels + [swapped(p, 1) for p in panels]

time: 62 us -> 56.8 us (0.916)
  waiting for transfers between devices: 12.5 us -> 5.24 us
  blocking collectives: 18.9 us -> 25.4 us
  Pallas kernels: 11.2 us -> 8.28 us
  local copies, waits for them, and re-layouts: 2.24 us -> 0 us
    all_to_all x1, waiting for transfers between devices: 6.82 us -> 0.01 us  [shards(): tables = lax.all_to_all(tables, 'gx', 0, 0, axis_index_groups=FAR_GROUPS)]
    all_to_all x1, blocking collectives: 18.9 us -> 25.4 us  [shards(): parts = lax.all_to_all(parts, 'gx', 0, 0, axis_index_groups=FAR_GROUPS)]
    pallas_call x1, Pallas kernels: 8.05 us -> 3.43 us  [contract(): pl.pallas_call(contract_kernel, out_shape=jax.ShapeDtypeStruct((FAR, PACK...]
    pallas_call x0 -> x1, Pallas kernels: none -> 1.63 us  [prepare(): pl.pallas_call(prepare_kernel, out_shape=(pltpu.VMEM((6, MODES, PLANE), j...]
    broadcast_in_dim x1 -> x0, local copies, waits for them, and re-layouts: 1.26 us -> none  [shards(): jnp.broadcast_to(pair_table, (FAR, ROWS))]
    slice x1 -> x0, local copies, waits for them, and re-layouts: 0.98 us -> none  [shards(): ahead = lax.ppermute(modes[:, :, :PLANE], 'gx', pairs)]
  transfers between devices with their start and end apart: 9 -> 9, of which waited for: 5 -> 4; matrix products, arithmetic and copies ran while one was open for 2% -> 0% of each run, Pallas kernels for 4% -> 4%
where the time goes in v3:
time: 56.8 us; the launch traced here: 56.5 us
  blocking collectives  25.4 us (45%)
  starting transfers between devices  16.9 us (30%)
  Pallas kernels  8.28 us (15%)
  waiting for transfers between devices  5.24 us (9%)
  between operations  0.72 us (1%)
    all_to_all x1, blocking collectives, shards(): parts = lax.all_to_all(parts, 'gx', 0, 0, axis_index_groups=FAR_GROUPS)  25.4 us
    all_to_all x1, starting transfers between devices, shards(): tables = lax.all_to_all(tables, 'gx', 0, 0, axis_index_groups=FAR_GROUPS)  11.2 us
    ppermute x7, starting transfers between devices, swapped(): lax.ppermute(value, 'gx', [(source, source ^ bits) for source in range(co...  5.6 us
    ppermute x7, waiting for transfers between devices, swapped(): lax.ppermute(value, 'gx', [(source, source ^ bits) for source in range(co...  5.23 us
    pallas_call x1, Pallas kernels, contract(): pl.pallas_call(contract_kernel, out_shape=jax.ShapeDtypeStruct((FAR, PACK...  3.43 us
    pallas_call x1, Pallas kernels, build_local(): pl.pallas_call(local_kernel, out_shape=(pltpu.VMEM((6 * MODES, LANES), jn...  1.92 us
    pallas_call x1, Pallas kernels, prepare(): pl.pallas_call(prepare_kernel, out_shape=(pltpu.VMEM((6, MODES, PLANE), j...  1.63 us
  transfers between devices with their start and end apart: 9, of which 4 were waited for; matrix products, arithmetic and copies ran while one was open for 0% of the time, Pallas kernels for 4%

profile of v3, /device:TPU:2, one launch (start us, length us, event | category | flops | bytes accessed | tf_op | source)
XLA Modules:
  0.0 56.5 jit_solution(18075341207016503681)
XLA Ops:
  0.0 1.6 %prepare.1 = (bf16[6,96,256]{2,1,0:T(8,128)(2,1)S(1)}, s32[16,16,128]{2,1,0:T(8,128)}) custom-call(s32[1,72]{1,0:T(1,128)} %bitcast.1, bf16[6,96,1024]{2,1,0:T(8,128)(2,1)} %modes_hbm.3), custom_call_target="tpu_custom_call" | custom-call | tf_op jit(solution)/shard_map/prepare/pallas_call | solution.py:41
  1.6 0.1 collective-permute-start
  1.7 11.2 %all-to-all-start = ((s32[16,16,128]{2,1,0:T(8,128)}), s32[16,16,128]{2,1,0:T(8,128)S(1)}, u32[]{:S(2)}, u32[]{:S(2)}) async-start(s32[16,16,128]{2,1,0:T(8,128)} %get-tuple-element.14), calls=%async_computation | async-start | bytes 262144 | tf_op jit(solution)/shard_map/all_to_all | solution.py:354
  13.6 1.9 %local_vectors.1 = (f32[576,128]{1,0:T(8,128)S(1)}, f32[24,128]{1,0:T(8,128)S(1)}, s32[8,128]{1,0:T(8,128)S(1)}) custom-call(s32[24]{0:T(128)} %sites_hbm.1, s32[1]{0:T(128)S(6)} %copy.6.counts_ref, bf16[6,96,1024]{2,1,0:T(8,128)(2,1)} %modes_hbm.3, f32[3,18,1024]{2,1,0:T(8,128)} %links_hbm.1), custom_call_target="tpu_custom_call" | custom-call | flops 200000000 | bytes 6000000 | tf_op jit(solution)/shard_map/local_vectors/pallas_call | solution.py:116
  15.5 0.0 collective-permute-done.ahead_ref
  15.5 0.5 build_panel.1.refs_0_
  16.0 1.6 %collective-permute-start.3 = (bf16[336,128]{1,0:T(8,128)(2,1)S(1)}, bf16[336,128]{1,0:T(8,128)(2,1)S(1)}, u32[]{:S(2)}, u32[]{:S(2)}) collective-permute-start(bf16[336,128]{1,0:T(8,128)(2,1)S(1)} %build_panel.1.refs_0_), channel_id=1, source_target_pairs={{0,6},{1,7},{2,4},{3,5},{4,2},{5,3},{6,0},{7,1},{8,14},{9,15},{10,... | collective-permute-start | bytes 258056 | tf_op jit(solution)/shard_map/ppermute | solution.py:346
  17.6 3.5 %collective-permute-start.2 = (bf16[336,128]{1,0:T(8,128)(2,1)S(1)}, bf16[336,128]{1,0:T(8,128)(2,1)S(1)}, u32[]{:S(2)}, u32[]{:S(2)}) collective-permute-start(bf16[336,128]{1,0:T(8,128)(2,1)S(1)} %build_panel.1.refs_0_), channel_id=1, source_target_pairs={{0,4},{1,5},{2,6},{3,7},{4,0},{5,1},{6,2},{7,3},{8,12},{9,13},{10,... | collective-permute-start | bytes 258056 | tf_op jit(solution)/shard_map/ppermute | solution.py:346
  21.1 0.0 collective-permute-start.1
  21.1 0.0 collective-permute-start.4
  21.1 0.0 collective-permute-done.3.refs_3_
  21.1 0.5 collective-permute-start.7
  21.6 2.8 %collective-permute-done.2.refs_2_ = bf16[336,128]{1,0:T(8,128)(2,1)S(1)} collective-permute-done((bf16[336,128]{1,0:T(8,128)(2,1)S(1)}, bf16[336,128]{1,0:T(8,128)(2,1)S(1)}, u32[]{:S(2)}, u32[]{:S(2)}) %collective-permute-start.2) | collective-permute-done | bytes 86048 | tf_op jit(solution)/shard_map/ppermute | solution.py:346
  24.4 0.0 collective-permute-start.6
  24.4 1.2 %collective-permute-done.1.refs_1_ = bf16[336,128]{1,0:T(8,128)(2,1)S(1)} collective-permute-done((bf16[336,128]{1,0:T(8,128)(2,1)S(1)}, bf16[336,128]{1,0:T(8,128)(2,1)S(1)}, u32[]{:S(2)}, u32[]{:S(2)}) %collective-permute-start.1) | collective-permute-done | bytes 86048 | tf_op jit(solution)/shard_map/ppermute | solution.py:346
  25.6 0.0 collective-permute-start.5
  25.6 0.0 all-to-all-done.refs_8_
  25.6 0.0 collective-permute-done.4.refs_4_
  25.6 0.0 collective-permute-done.7.refs_7_
  25.6 0.1 collective-permute-done.6.refs_6_
  25.7 1.2 %collective-permute-done.5.refs_5_ = bf16[336,128]{1,0:T(8,128)(2,1)S(1)} collective-permute-done((bf16[336,128]{1,0:T(8,128)(2,1)S(1)}, bf16[336,128]{1,0:T(8,128)(2,1)S(1)}, u32[]{:S(2)}, u32[]{:S(2)}) %collective-permute-start.5) | collective-permute-done | bytes 86048 | tf_op jit(solution)/shard_map/ppermute | solution.py:346
  26.9 3.4 %contract_pairs.1 = bf16[16,112,128]{2,1,0:T(8,128)(2,1)S(1)} custom-call(bf16[336,128]{1,0:T(8,128)(2,1)S(1)} %build_panel.1.refs_0_, bf16[336,128]{1,0:T(8,128)(2,1)S(1)} %collective-permute-done.1.refs_1_, bf16[336,128]{1,0:T(8,128)(2,1)S(1)} %collective-permute-done.2.refs_2_, bf16[336,128]{1,0:T(8,128)(2,1)S(1)} %collective-permute-done.3.refs_3_, ...), custom_call_target="tpu_custom_call" | custom-call | tf_op jit(solution)/shard_map/contract_pairs/pallas_call | solution.py:301
  30.3 25.4 %all_to_all.10.refs_0_ = bf16[16,112,128]{2,1,0:T(8,128)(2,1)S(1)} all-to-all(bf16[16,112,128]{2,1,0:T(8,128)(2,1)S(1)} %contract_pairs.1), channel_id=1, replica_groups={{0,8,16,24,32,40,48,56,64,72,80,88,96,104,112,120},{1,9,17,25,33,41,49,..., dimensions={0} | all-to-all | bytes 917504 | tf_op jit(solution)/shard_map/all_to_all | solution.py:361
  55.7 0.8 %add_up.1 = f32[72,192]{1,0:T(8,128)} custom-call(bf16[16,112,128]{2,1,0:T(8,128)(2,1)S(1)} %all_to_all.10.refs_0_), custom_call_target="tpu_custom_call" | custom-call | tf_op jit(solution)/shard_map/add_up/pallas_call | solution.py:334
Async XLA Ops:
  1.6 13.9 %collective-permute-start = (bf16[6,96,256]{2,1,0:T(8,128)(2,1)S(1)}, bf16[6,96,256]{2,1,0:T(8,128)(2,1)S(1)}, u32[]{:S(2)}, u32[]{:S(2)}) collective-permute-start(bf16[6,96,256]{2,1,0:T(8,128)(2,1)S(1)} %get-tuple-element.13), channel_id=1, source_target_pairs={{0,127},{1,0},{2,1},{3,2},{4,3},{5,4},{6,5},{7,6},{8,7},{9,8},{10,... | collective-permute-start | bytes 884744 | tf_op jit(solution)/shard_map/ppermute | solution.py:353
  1.7 23.9 %all-to-all-start = ((s32[16,16,128]{2,1,0:T(8,128)}), s32[16,16,128]{2,1,0:T(8,128)S(1)}, u32[]{:S(2)}, u32[]{:S(2)}) async-start(s32[16,16,128]{2,1,0:T(8,128)} %get-tuple-element.14), calls=%async_computation | async-start | bytes 262144 | tf_op jit(solution)/shard_map/all_to_all | solution.py:354
  16.0 5.1 %collective-permute-start.3 = (bf16[336,128]{1,0:T(8,128)(2,1)S(1)}, bf16[336,128]{1,0:T(8,128)(2,1)S(1)}, u32[]{:S(2)}, u32[]{:S(2)}) collective-permute-start(bf16[336,128]{1,0:T(8,128)(2,1)S(1)} %build_panel.1.refs_0_), channel_id=1, source_target_pairs={{0,6},{1,7},{2,4},{3,5},{4,2},{5,3},{6,0},{7,1},{8,14},{9,15},{10,... | collective-permute-start | bytes 258056 | tf_op jit(solution)/shard_map/ppermute | solution.py:346
  17.6 6.8 %collective-permute-start.2 = (bf16[336,128]{1,0:T(8,128)(2,1)S(1)}, bf16[336,128]{1,0:T(8,128)(2,1)S(1)}, u32[]{:S(2)}, u32[]{:S(2)}) collective-permute-start(bf16[336,128]{1,0:T(8,128)(2,1)S(1)} %build_panel.1.refs_0_), channel_id=1, source_target_pairs={{0,4},{1,5},{2,6},{3,7},{4,0},{5,1},{6,2},{7,3},{8,12},{9,13},{10,... | collective-permute-start | bytes 258056 | tf_op jit(solution)/shard_map/ppermute | solution.py:346
  21.1 4.5 %collective-permute-start.1 = (bf16[336,128]{1,0:T(8,128)(2,1)S(1)}, bf16[336,128]{1,0:T(8,128)(2,1)S(1)}, u32[]{:S(2)}, u32[]{:S(2)}) collective-permute-start(bf16[336,128]{1,0:T(8,128)(2,1)S(1)} %build_panel.1.refs_0_), channel_id=1, source_target_pairs={{0,2},{1,3},{2,0},{3,1},{4,6},{5,7},{6,4},{7,5},{8,10},{9,11},{10,... | collective-permute-start | bytes 258056 | tf_op jit(solution)/shard_map/ppermute | solution.py:346
  21.1 4.5 %collective-permute-start.4 = (bf16[336,128]{1,0:T(8,128)(2,1)S(1)}, bf16[336,128]{1,0:T(8,128)(2,1)S(1)}, u32[]{:S(2)}, u32[]{:S(2)}) collective-permute-start(bf16[336,128]{1,0:T(8,128)(2,1)S(1)} %build_panel.1.refs_0_), channel_id=1, source_target_pairs={{0,1},{1,0},{2,3},{3,2},{4,5},{5,4},{6,7},{7,6},{8,9},{9,8},{10,11... | collective-permute-start | bytes 258056 | tf_op jit(solution)/shard_map/ppermute | solution.py:346
  21.1 4.5 %collective-permute-start.7 = (bf16[336,128]{1,0:T(8,128)(2,1)S(1)}, bf16[336,128]{1,0:T(8,128)(2,1)S(1)}, u32[]{:S(2)}, u32[]{:S(2)}) collective-permute-start(bf16[336,128]{1,0:T(8,128)(2,1)S(1)} %collective-permute-done.3.refs_3_), channel_id=1, source_target_pairs={{0,1},{1,0},{2,3},{3,2},{4,5},{5,4},{6,7},{7,6},{8,9},{9,8},{10,11... | collective-permute-start | bytes 258056 | tf_op jit(solution)/shard_map/ppermute | solution.py:346
  24.4 1.3 %collective-permute-start.6 = (bf16[336,128]{1,0:T(8,128)(2,1)S(1)}, bf16[336,128]{1,0:T(8,128)(2,1)S(1)}, u32[]{:S(2)}, u32[]{:S(2)}) collective-permute-start(bf16[336,128]{1,0:T(8,128)(2,1)S(1)} %collective-permute-done.2.refs_2_), channel_id=1, source_target_pairs={{0,1},{1,0},{2,3},{3,2},{4,5},{5,4},{6,7},{7,6},{8,9},{9,8},{10,11... | collective-permute-start | bytes 258056 | tf_op jit(solution)/shard_map/ppermute | solution.py:346
  25.6 1.3 %collective-permute-start.5 = (bf16[336,128]{1,0:T(8,128)(2,1)S(1)}, bf16[336,128]{1,0:T(8,128)(2,1)S(1)}, u32[]{:S(2)}, u32[]{:S(2)}) collective-permute-start(bf16[336,128]{1,0:T(8,128)(2,1)S(1)} %collective-permute-done.1.refs_1_), channel_id=1, source_target_pairs={{0,1},{1,0},{2,3},{3,2},{4,5},{5,4},{6,7},{7,6},{8,9},{9,8},{10,11... | collective-permute-start | bytes 258056 | tf_op jit(solution)/shard_map/ppermute | solution.py:346

commit v4 on v3

--- a/solution.py
+++ b/solution.py
@@ -24,50 +24,23 @@
     return pltpu.with_memory_space_constraint(value, pltpu.HBM)
 
 
-def prepare_kernel(table_hbm, modes_hbm, plane_ref, tables_ref, table_ref, sems):
-    small = pltpu.make_async_copy(table_hbm, table_ref, sems.at[0])
-    small.start()
-    copy = pltpu.make_async_copy(modes_hbm.at[:, :, pl.ds(0, PLANE)], plane_ref, sems.at[1])
-    copy.start()
-    small.wait()
-    row = jnp.concatenate([table_ref[...], jnp.zeros((1, LANES - ROWS), jnp.int32)], axis=1)
-    for g in range(FAR):
-        tables_ref[g] = jnp.broadcast_to(row, (16, LANES))
-    copy.wait()
-
-
-def prepare(modes, pair_table):
-    vmem = pl.BlockSpec(memory_space=pltpu.VMEM)
-    return pl.pallas_call(
-        prepare_kernel,
-        out_shape=(
-            pltpu.VMEM((6, MODES, PLANE), jnp.bfloat16),
-            pltpu.VMEM((FAR, 16, LANES), jnp.int32),
-        ),
-        in_specs=[pl.BlockSpec(memory_space=pltpu.HBM)] * 2,
-        out_specs=(vmem, vmem),
-        scratch_shapes=[pltpu.VMEM((1, ROWS), jnp.int32), pltpu.SemaphoreType.DMA((2,))],
-        compiler_params=pltpu.CompilerParams(vmem_limit_bytes=8 << 20),
-        name="prepare",
-    )(pinned(pair_table.reshape(1, ROWS)), pinned(modes))
-
-
 def local_kernel(
-    sites_hbm, counts_ref, modes_hbm, links_hbm, vec_ref, link_ref, marks_ref,
-    sites_ref, modes_ref, links_ref, rows_ref, sems,
+    table_hbm, sites_hbm, modes_hbm, links_hbm, plane_ref, tables_ref, vec_ref, link_ref, marks_ref,
+    table_ref, sites_ref, modes_ref, links_ref, rows_ref, sems,
 ):
     copies = [
         pltpu.make_async_copy(sites_hbm, sites_ref, sems.at[0]),
         pltpu.make_async_copy(links_hbm, links_ref, sems.at[1]),
     ] + [pltpu.make_async_copy(modes_hbm.at[c], modes_ref.at[c], sems.at[2 + c]) for c in range(6)]
+    table_copy = pltpu.make_async_copy(table_hbm, table_ref, sems.at[8])
+    table_copy.start()
     for copy in copies:
         copy.start()
     lane = lax.broadcasted_iota(jnp.int32, (1, LANES), 1)
     slot = jnp.where(lane < SLOTS, lane, jnp.where(lane < 2 * SLOTS, lane - SLOTS, lane - 2 * SLOTS))
     copies[0].wait()
-    site = jnp.zeros((1, LANES), jnp.int32)
-    for s in range(SLOTS):
-        site = jnp.where(slot == s, sites_ref[s], site)
+    listed = jnp.concatenate([sites_ref[...], jnp.zeros((1, LANES - SLOTS), jnp.int32)], axis=1)
+    site = listed + pltpu.roll(listed, SLOTS, 1) + pltpu.roll(listed, 2 * SLOTS, 1)
     z = site & (LZ - 1)
     y = (site >> 4) & (LY - 1)
     base = site - (y << 4) - z
@@ -84,7 +57,11 @@
     near = jnp.where(used, near, -1)
     at = jnp.where(used, site, -1)
     marks_ref[0:1, :] = near - SITES
-    marks_ref[1:2, :] = jnp.where(slot < counts_ref[0], 1, 0)
+    marks_ref[1:2, :] = slot
+    table_copy.wait()
+    pairs = jnp.concatenate([table_ref[...], jnp.zeros((1, LANES - ROWS), jnp.int32)], axis=1)
+    for g in range(FAR):
+        tables_ref[g] = jnp.broadcast_to(pairs, (16, LANES))
     row = lax.broadcasted_iota(jnp.int32, (SITES, LANES), 0)
     pick = jnp.where(row == near, 1.0, 0.0).astype(jnp.bfloat16)
     pick_site = jnp.where(row == at, 1.0, 0.0).astype(jnp.bfloat16)
@@ -106,41 +83,44 @@
     )
     for c in range(6):
         copies[2 + c].wait()
+    plane_ref[...] = modes_ref[:, :, 0:PLANE]
     field = modes_ref[...].reshape(6 * MODES, SITES)
     vec_ref[...] = jnp.dot(field, pick, preferred_element_type=jnp.float32)
 
 
-def build_local(sites, counts, modes, links):
+def build_local(pair_table, sites, modes, links):
     vmem = pl.BlockSpec(memory_space=pltpu.VMEM)
     hbm = pl.BlockSpec(memory_space=pltpu.HBM)
     return pl.pallas_call(
         local_kernel,
         out_shape=(
+            pltpu.VMEM((6, MODES, PLANE), jnp.bfloat16),
+            pltpu.VMEM((FAR, 16, LANES), jnp.int32),
             pltpu.VMEM((6 * MODES, LANES), jnp.float32),
             pltpu.VMEM((24, LANES), jnp.float32),
             pltpu.VMEM((8, LANES), jnp.int32),
         ),
-        in_specs=[hbm, pl.BlockSpec(memory_space=pltpu.SMEM), hbm, hbm],
-        out_specs=(vmem, vmem, vmem),
+        in_specs=[hbm] * 4,
+        out_specs=(vmem,) * 5,
         scratch_shapes=[
-            pltpu.SMEM((SLOTS,), jnp.int32),
+            pltpu.VMEM((1, ROWS), jnp.int32),
+            pltpu.VMEM((1, SLOTS), jnp.int32),
             pltpu.VMEM((6, MODES, SITES), jnp.bfloat16),
             pltpu.VMEM((3, 18, SITES), jnp.float32),
             pltpu.VMEM((72, SITES), jnp.float32),
-            pltpu.SemaphoreType.DMA((8,)),
+            pltpu.SemaphoreType.DMA((9,)),
         ],
         compiler_params=pltpu.CompilerParams(vmem_limit_bytes=16 << 20),
-        cost_estimate=pl.CostEstimate(flops=200_000_000, bytes_accessed=6_000_000, transcendentals=0),
         name="local_vectors",
-    )(pinned(sites), counts, pinned(modes), pinned(links))
-
-
-def build_kernel(vec_ref, link_ref, marks_ref, ahead_ref, out_ref):
+    )(pinned(pair_table.reshape(1, ROWS)), pinned(sites.reshape(1, SLOTS)), pinned(modes), pinned(links))
+
+
+def build_kernel(counts_ref, vec_ref, link_ref, marks_ref, ahead_ref, out_ref):
     row = lax.broadcasted_iota(jnp.int32, (PLANE, LANES), 0)
     pick_ahead = jnp.where(row == marks_ref[0:1, :], 1.0, 0.0).astype(jnp.bfloat16)
     ahead = ahead_ref[...].reshape(6 * MODES, PLANE)
     vec = vec_ref[...] + jnp.dot(ahead, pick_ahead, preferred_element_type=jnp.float32)
-    live = marks_ref[1:2, :] > 0
+    live = marks_ref[1:2, :] < counts_ref[0]
     link = link_ref[...]
     blank = jnp.zeros((LANES - MODES, LANES), jnp.float32)
     turned = []
@@ -169,16 +149,16 @@
     out_ref[...] = jnp.where(lane < MODES, main, spread).astype(jnp.bfloat16)
 
 
-def build(vec, link, marks, ahead):
+def build(counts, vec, link, marks, ahead):
     vmem = pl.BlockSpec(memory_space=pltpu.VMEM)
     return pl.pallas_call(
         build_kernel,
         out_shape=jax.ShapeDtypeStruct((WIRE, LANES), jnp.bfloat16),
-        in_specs=[vmem] * 4,
+        in_specs=[pl.BlockSpec(memory_space=pltpu.SMEM)] + [vmem] * 4,
         out_specs=vmem,
         compiler_params=pltpu.CompilerParams(vmem_limit_bytes=16 << 20),
         name="build_panel",
-    )(vec, link, marks, ahead)
+    )(counts, vec, link, marks, ahead)
 
 
 TILES = ((0, 256), (256, 256), (512, 256), (768, 256), (1024, 128))
@@ -349,11 +329,10 @@
 def shards(modes, links, sites, counts, pair_table):
     count = lax.axis_size("gx")
     pairs = [(source, (source - 1) % count) for source in range(count)]
-    plane, tables = prepare(modes, pair_table)
+    plane, tables, vec, link, marks = build_local(pair_table, sites, modes, links)
     ahead = lax.ppermute(plane, "gx", pairs)
     tables = lax.all_to_all(tables, "gx", 0, 0, axis_index_groups=FAR_GROUPS)
-    vec, link, marks = build_local(sites, counts, modes, links)
-    panel = build(vec, link, marks, ahead)
+    panel = build(counts, vec, link, marks, ahead)
     others = [swapped(panel, bits) for bits in (2, 4, 6)]
     panels = [panel] + others
     panels = panels + [swapped(p, 1) for p in panels]

time: 56.8 us -> 55.3 us (0.974)
  blocking collectives: 25.4 us -> 23.9 us
  starting transfers between devices: 16.9 us -> 18.4 us
  Pallas kernels: 8.28 us -> 6.87 us
    all_to_all x1, blocking collectives: 25.4 us -> 23.9 us  [shards(): parts = lax.all_to_all(parts, 'gx', 0, 0, axis_index_groups=FAR_GROUPS)]
    ppermute x7, starting transfers between devices: 5.6 us -> 7.11 us  [swapped(): lax.ppermute(value, 'gx', [(source, source ^ bits) for source in range(co...]
    pallas_call x2 -> x1, Pallas kernels: 3.55 us -> 2.13 us  [build_local(): pl.pallas_call(local_kernel, out_shape=(pltpu.VMEM((6, MODES, PLANE), jnp...]
  transfers between devices with their start and end apart: 9 -> 9, of which waited for: 4 -> 3; matrix products, arithmetic and copies ran while one was open for 0% -> 0% of each run, Pallas kernels for 4% -> 1%
where the time goes in v4:
time: 55.3 us; the launch traced here: 55.1 us
  blocking collectives  23.9 us (43%)
  starting transfers between devices  18.4 us (33%)
  Pallas kernels  6.87 us (12%)
  waiting for transfers between devices  5.23 us (9%)
  between operations  0.72 us (1%)
    all_to_all x1, blocking collectives, shards(): parts = lax.all_to_all(parts, 'gx', 0, 0, axis_index_groups=FAR_GROUPS)  23.9 us
    all_to_all x1, starting transfers between devices, shards(): tables = lax.all_to_all(tables, 'gx', 0, 0, axis_index_groups=FAR_GROUPS)  11.2 us
    ppermute x7, starting transfers between devices, swapped(): lax.ppermute(value, 'gx', [(source, source ^ bits) for source in range(co...  7.11 us
    ppermute x7, waiting for transfers between devices, swapped(): lax.ppermute(value, 'gx', [(source, source ^ bits) for source in range(co...  5.22 us
    pallas_call x1, Pallas kernels, contract(): pl.pallas_call(contract_kernel, out_shape=jax.ShapeDtypeStruct((FAR, PACK...  3.43 us
    pallas_call x1, Pallas kernels, build_local(): pl.pallas_call(local_kernel, out_shape=(pltpu.VMEM((6, MODES, PLANE), jnp...  2.13 us
  transfers between devices with their start and end apart: 9, of which 3 were waited for; matrix products, arithmetic and copies ran while one was open for 0% of the time, Pallas kernels for 1%

profile of v4, /device:TPU:2, one launch (start us, length us, event | category | flops | bytes accessed | tf_op | source)
XLA Modules:
  0.0 55.1 jit_solution(6359843599915373298)
XLA Ops:
  0.0 2.1 %local_vectors.1 = (bf16[6,96,256]{2,1,0:T(8,128)(2,1)S(1)}, s32[16,16,128]{2,1,0:T(8,128)}, f32[576,128]{1,0:T(8,128)S(1)}, f32[24,128]{1,0:T(8,128)S(1)}, s32[8,128]{1,0:T(8,128)S(1)}) custom-call(s32[1,72]{1,0:T(1,128)} %bitcast.2, s32[1,24]{1,0:T(1,128)} %bitcast.3, bf16[6,96,1024]{2,1,0:T(8,128)(2,1)} %modes_hbm.1, f32[3,18,1024]{2,1,0:T(8,128)} %links_hbm.1), custom_call_target="tpu_custom_call" | custom-call | tf_op jit(solution)/shard_map/local_vectors/pallas_call | solution.py:94
  2.1 0.1 collective-permute-start
  2.2 11.2 %all-to-all-start = ((s32[16,16,128]{2,1,0:T(8,128)}), s32[16,16,128]{2,1,0:T(8,128)S(1)}, u32[]{:S(2)}, u32[]{:S(2)}) async-start(s32[16,16,128]{2,1,0:T(8,128)} %get-tuple-element.14), calls=%async_computation | async-start | bytes 262144 | tf_op jit(solution)/shard_map/all_to_all | solution.py:334
  14.1 0.0 collective-permute-done.ahead_ref
  14.1 0.5 build_panel.1.refs_0_
  14.6 1.6 %collective-permute-start.3 = (bf16[336,128]{1,0:T(8,128)(2,1)S(1)}, bf16[336,128]{1,0:T(8,128)(2,1)S(1)}, u32[]{:S(2)}, u32[]{:S(2)}) collective-permute-start(bf16[336,128]{1,0:T(8,128)(2,1)S(1)} %build_panel.1.refs_0_), channel_id=1, source_target_pairs={{0,6},{1,7},{2,4},{3,5},{4,2},{5,3},{6,0},{7,1},{8,14},{9,15},{10,... | collective-permute-start | bytes 258056 | tf_op jit(solution)/shard_map/ppermute | solution.py:326
  16.2 5.0 %collective-permute-start.2 = (bf16[336,128]{1,0:T(8,128)(2,1)S(1)}, bf16[336,128]{1,0:T(8,128)(2,1)S(1)}, u32[]{:S(2)}, u32[]{:S(2)}) collective-permute-start(bf16[336,128]{1,0:T(8,128)(2,1)S(1)} %build_panel.1.refs_0_), channel_id=1, source_target_pairs={{0,4},{1,5},{2,6},{3,7},{4,0},{5,1},{6,2},{7,3},{8,12},{9,13},{10,... | collective-permute-start | bytes 258056 | tf_op jit(solution)/shard_map/ppermute | solution.py:326
  21.2 0.0 collective-permute-start.1
  21.2 0.0 collective-permute-start.4
  21.2 0.0 collective-permute-done.3.refs_3_
  21.2 0.5 collective-permute-start.7
  21.7 1.9 %collective-permute-done.2.refs_2_ = bf16[336,128]{1,0:T(8,128)(2,1)S(1)} collective-permute-done((bf16[336,128]{1,0:T(8,128)(2,1)S(1)}, bf16[336,128]{1,0:T(8,128)(2,1)S(1)}, u32[]{:S(2)}, u32[]{:S(2)}) %collective-permute-start.2) | collective-permute-done | bytes 86048 | tf_op jit(solution)/shard_map/ppermute | solution.py:326
  23.7 0.0 collective-permute-start.6
  23.7 2.0 %collective-permute-done.1.refs_1_ = bf16[336,128]{1,0:T(8,128)(2,1)S(1)} collective-permute-done((bf16[336,128]{1,0:T(8,128)(2,1)S(1)}, bf16[336,128]{1,0:T(8,128)(2,1)S(1)}, u32[]{:S(2)}, u32[]{:S(2)}) %collective-permute-start.1) | collective-permute-done | bytes 86048 | tf_op jit(solution)/shard_map/ppermute | solution.py:326
  25.7 0.0 collective-permute-start.5
  25.7 0.0 all-to-all-done.refs_8_
  25.7 0.0 collective-permute-done.4.refs_4_
  25.7 0.0 collective-permute-done.7.refs_7_
  25.7 0.0 collective-permute-done.6.refs_6_
  25.7 1.2 %collective-permute-done.5.refs_5_ = bf16[336,128]{1,0:T(8,128)(2,1)S(1)} collective-permute-done((bf16[336,128]{1,0:T(8,128)(2,1)S(1)}, bf16[336,128]{1,0:T(8,128)(2,1)S(1)}, u32[]{:S(2)}, u32[]{:S(2)}) %collective-permute-start.5) | collective-permute-done | bytes 86048 | tf_op jit(solution)/shard_map/ppermute | solution.py:326
  27.0 3.4 %contract_pairs.1 = bf16[16,112,128]{2,1,0:T(8,128)(2,1)S(1)} custom-call(bf16[336,128]{1,0:T(8,128)(2,1)S(1)} %build_panel.1.refs_0_, bf16[336,128]{1,0:T(8,128)(2,1)S(1)} %collective-permute-done.1.refs_1_, bf16[336,128]{1,0:T(8,128)(2,1)S(1)} %collective-permute-done.2.refs_2_, bf16[336,128]{1,0:T(8,128)(2,1)S(1)} %collective-permute-done.3.refs_3_, ...), custom_call_target="tpu_custom_call" | custom-call | tf_op jit(solution)/shard_map/contract_pairs/pallas_call | solution.py:281
  30.4 23.9 %all_to_all.10.refs_0_ = bf16[16,112,128]{2,1,0:T(8,128)(2,1)S(1)} all-to-all(bf16[16,112,128]{2,1,0:T(8,128)(2,1)S(1)} %contract_pairs.1), channel_id=1, replica_groups={{0,8,16,24,32,40,48,56,64,72,80,88,96,104,112,120},{1,9,17,25,33,41,49,..., dimensions={0} | all-to-all | bytes 917504 | tf_op jit(solution)/shard_map/all_to_all | solution.py:340
  54.3 0.8 %add_up.1 = f32[72,192]{1,0:T(8,128)} custom-call(bf16[16,112,128]{2,1,0:T(8,128)(2,1)S(1)} %all_to_all.10.refs_0_), custom_call_target="tpu_custom_call" | custom-call | tf_op jit(solution)/shard_map/add_up/pallas_call | solution.py:314
Async XLA Ops:
  2.1 12.0 %collective-permute-start = (bf16[6,96,256]{2,1,0:T(8,128)(2,1)S(1)}, bf16[6,96,256]{2,1,0:T(8,128)(2,1)S(1)}, u32[]{:S(2)}, u32[]{:S(2)}) collective-permute-start(bf16[6,96,256]{2,1,0:T(8,128)(2,1)S(1)} %get-tuple-element.13), channel_id=1, source_target_pairs={{0,127},{1,0},{2,1},{3,2},{4,3},{5,4},{6,5},{7,6},{8,7},{9,8},{10,... | collective-permute-start | bytes 884744 | tf_op jit(solution)/shard_map/ppermute | solution.py:333
  2.2 23.4 %all-to-all-start = ((s32[16,16,128]{2,1,0:T(8,128)}), s32[16,16,128]{2,1,0:T(8,128)S(1)}, u32[]{:S(2)}, u32[]{:S(2)}) async-start(s32[16,16,128]{2,1,0:T(8,128)} %get-tuple-element.14), calls=%async_computation | async-start | bytes 262144 | tf_op jit(solution)/shard_map/all_to_all | solution.py:334
  14.6 6.6 %collective-permute-start.3 = (bf16[336,128]{1,0:T(8,128)(2,1)S(1)}, bf16[336,128]{1,0:T(8,128)(2,1)S(1)}, u32[]{:S(2)}, u32[]{:S(2)}) collective-permute-start(bf16[336,128]{1,0:T(8,128)(2,1)S(1)} %build_panel.1.refs_0_), channel_id=1, source_target_pairs={{0,6},{1,7},{2,4},{3,5},{4,2},{5,3},{6,0},{7,1},{8,14},{9,15},{10,... | collective-permute-start | bytes 258056 | tf_op jit(solution)/shard_map/ppermute | solution.py:326
  16.2 7.5 %collective-permute-start.2 = (bf16[336,128]{1,0:T(8,128)(2,1)S(1)}, bf16[336,128]{1,0:T(8,128)(2,1)S(1)}, u32[]{:S(2)}, u32[]{:S(2)}) collective-permute-start(bf16[336,128]{1,0:T(8,128)(2,1)S(1)} %build_panel.1.refs_0_), channel_id=1, source_target_pairs={{0,4},{1,5},{2,6},{3,7},{4,0},{5,1},{6,2},{7,3},{8,12},{9,13},{10,... | collective-permute-start | bytes 258056 | tf_op jit(solution)/shard_map/ppermute | solution.py:326
  21.2 4.5 %collective-permute-start.1 = (bf16[336,128]{1,0:T(8,128)(2,1)S(1)}, bf16[336,128]{1,0:T(8,128)(2,1)S(1)}, u32[]{:S(2)}, u32[]{:S(2)}) collective-permute-start(bf16[336,128]{1,0:T(8,128)(2,1)S(1)} %build_panel.1.refs_0_), channel_id=1, source_target_pairs={{0,2},{1,3},{2,0},{3,1},{4,6},{5,7},{6,4},{7,5},{8,10},{9,11},{10,... | collective-permute-start | bytes 258056 | tf_op jit(solution)/shard_map/ppermute | solution.py:326
  21.2 4.5 %collective-permute-start.4 = (bf16[336,128]{1,0:T(8,128)(2,1)S(1)}, bf16[336,128]{1,0:T(8,128)(2,1)S(1)}, u32[]{:S(2)}, u32[]{:S(2)}) collective-permute-start(bf16[336,128]{1,0:T(8,128)(2,1)S(1)} %build_panel.1.refs_0_), channel_id=1, source_target_pairs={{0,1},{1,0},{2,3},{3,2},{4,5},{5,4},{6,7},{7,6},{8,9},{9,8},{10,11... | collective-permute-start | bytes 258056 | tf_op jit(solution)/shard_map/ppermute | solution.py:326
  21.2 4.5 %collective-permute-start.7 = (bf16[336,128]{1,0:T(8,128)(2,1)S(1)}, bf16[336,128]{1,0:T(8,128)(2,1)S(1)}, u32[]{:S(2)}, u32[]{:S(2)}) collective-permute-start(bf16[336,128]{1,0:T(8,128)(2,1)S(1)} %collective-permute-done.3.refs_3_), channel_id=1, source_target_pairs={{0,1},{1,0},{2,3},{3,2},{4,5},{5,4},{6,7},{7,6},{8,9},{9,8},{10,11... | collective-permute-start | bytes 258056 | tf_op jit(solution)/shard_map/ppermute | solution.py:326
  23.7 2.0 %collective-permute-start.6 = (bf16[336,128]{1,0:T(8,128)(2,1)S(1)}, bf16[336,128]{1,0:T(8,128)(2,1)S(1)}, u32[]{:S(2)}, u32[]{:S(2)}) collective-permute-start(bf16[336,128]{1,0:T(8,128)(2,1)S(1)} %collective-permute-done.2.refs_2_), channel_id=1, source_target_pairs={{0,1},{1,0},{2,3},{3,2},{4,5},{5,4},{6,7},{7,6},{8,9},{9,8},{10,11... | collective-permute-start | bytes 258056 | tf_op jit(solution)/shard_map/ppermute | solution.py:326
  25.7 1.3 %collective-permute-start.5 = (bf16[336,128]{1,0:T(8,128)(2,1)S(1)}, bf16[336,128]{1,0:T(8,128)(2,1)S(1)}, u32[]{:S(2)}, u32[]{:S(2)}) collective-permute-start(bf16[336,128]{1,0:T(8,128)(2,1)S(1)} %collective-permute-done.1.refs_1_), channel_id=1, source_target_pairs={{0,1},{1,0},{2,3},{3,2},{4,5},{5,4},{6,7},{7,6},{8,9},{9,8},{10,11... | collective-permute-start | bytes 258056 | tf_op jit(solution)/shard_map/ppermute | solution.py:326

commit v5 on v4

--- a/solution.py
+++ b/solution.py
@@ -26,7 +26,7 @@
 
 def local_kernel(
     table_hbm, sites_hbm, modes_hbm, links_hbm, plane_ref, tables_ref, vec_ref, link_ref, marks_ref,
-    table_ref, sites_ref, modes_ref, links_ref, rows_ref, sems,
+    table_ref, spread_ref, sites_ref, modes_ref, links_ref, rows_ref, sems,
 ):
     copies = [
         pltpu.make_async_copy(sites_hbm, sites_ref, sems.at[0]),
@@ -61,7 +61,9 @@
     table_copy.wait()
     pairs = jnp.concatenate([table_ref[...], jnp.zeros((1, LANES - ROWS), jnp.int32)], axis=1)
     for g in range(FAR):
-        tables_ref[g] = jnp.broadcast_to(pairs, (16, LANES))
+        spread_ref[g] = jnp.broadcast_to(pairs, (16, LANES))
+    out_copy = pltpu.make_async_copy(spread_ref, tables_ref, sems.at[9])
+    out_copy.start()
     row = lax.broadcasted_iota(jnp.int32, (SITES, LANES), 0)
     pick = jnp.where(row == near, 1.0, 0.0).astype(jnp.bfloat16)
     pick_site = jnp.where(row == at, 1.0, 0.0).astype(jnp.bfloat16)
@@ -86,6 +88,7 @@
     plane_ref[...] = modes_ref[:, :, 0:PLANE]
     field = modes_ref[...].reshape(6 * MODES, SITES)
     vec_ref[...] = jnp.dot(field, pick, preferred_element_type=jnp.float32)
+    out_copy.wait()
 
 
 def build_local(pair_table, sites, modes, links):
@@ -95,20 +98,21 @@
         local_kernel,
         out_shape=(
             pltpu.VMEM((6, MODES, PLANE), jnp.bfloat16),
-            pltpu.VMEM((FAR, 16, LANES), jnp.int32),
+            pltpu.HBM((FAR, 16, LANES), jnp.int32),
             pltpu.VMEM((6 * MODES, LANES), jnp.float32),
             pltpu.VMEM((24, LANES), jnp.float32),
             pltpu.VMEM((8, LANES), jnp.int32),
         ),
         in_specs=[hbm] * 4,
-        out_specs=(vmem,) * 5,
+        out_specs=(vmem, hbm, vmem, vmem, vmem),
         scratch_shapes=[
             pltpu.VMEM((1, ROWS), jnp.int32),
+            pltpu.VMEM((FAR, 16, LANES), jnp.int32),
             pltpu.VMEM((1, SLOTS), jnp.int32),
             pltpu.VMEM((6, MODES, SITES), jnp.bfloat16),
             pltpu.VMEM((3, 18, SITES), jnp.float32),
             pltpu.VMEM((72, SITES), jnp.float32),
-            pltpu.SemaphoreType.DMA((9,)),
+            pltpu.SemaphoreType.DMA((10,)),
         ],
         compiler_params=pltpu.CompilerParams(vmem_limit_bytes=16 << 20),
         name="local_vectors",

time: 55.3 us -> 55.2 us (level)
  no operation moved by 1% of the time
where the time goes in v5:
time: 55.2 us; the launch traced here: 55 us
  blocking collectives  23.9 us (43%)
  starting transfers between devices  18.4 us (33%)
  Pallas kernels  6.72 us (12%)
  waiting for transfers between devices  5.23 us (9%)
  between operations  0.72 us (1%)
    all_to_all x1, blocking collectives, shards(): parts = lax.all_to_all(parts, 'gx', 0, 0, axis_index_groups=FAR_GROUPS)  23.9 us
    all_to_all x1, starting transfers between devices, shards(): tables = lax.all_to_all(tables, 'gx', 0, 0, axis_index_groups=FAR_GROUPS)  11.2 us
    ppermute x7, starting transfers between devices, swapped(): lax.ppermute(value, 'gx', [(source, source ^ bits) for source in range(co...  7.12 us
    ppermute x7, waiting for transfers between devices, swapped(): lax.ppermute(value, 'gx', [(source, source ^ bits) for source in range(co...  5.22 us
    pallas_call x1, Pallas kernels, contract(): pl.pallas_call(contract_kernel, out_shape=jax.ShapeDtypeStruct((FAR, PACK...  3.43 us
    pallas_call x1, Pallas kernels, build_local(): pl.pallas_call(local_kernel, out_shape=(pltpu.VMEM((6, MODES, PLANE), jnp...  1.98 us
  transfers between devices with their start and end apart: 9, of which 3 were waited for; matrix products, arithmetic and copies ran while one was open for 0% of the time, Pallas kernels for 1%

profile of v5, /device:TPU:2, one launch (start us, length us, event | category | flops | bytes accessed | tf_op | source)
XLA Modules:
  0.0 55.0 jit_solution(11974201025338462183)
XLA Ops:
  0.0 2.0 %local_vectors.1 = (bf16[6,96,256]{2,1,0:T(8,128)(2,1)S(1)}, s32[16,16,128]{2,1,0:T(8,128)}, f32[576,128]{1,0:T(8,128)S(1)}, f32[24,128]{1,0:T(8,128)S(1)}, s32[8,128]{1,0:T(8,128)S(1)}) custom-call(s32[1,72]{1,0:T(1,128)} %bitcast.2, s32[1,24]{1,0:T(1,128)} %bitcast.3, bf16[6,96,1024]{2,1,0:T(8,128)(2,1)} %modes_hbm.1, f32[3,18,1024]{2,1,0:T(8,128)} %links_hbm.1), custom_call_target="tpu_custom_call" | custom-call | tf_op jit(solution)/shard_map/local_vectors/pallas_call | solution.py:97
  2.0 0.1 collective-permute-start
  2.1 11.2 %all-to-all-start = ((s32[16,16,128]{2,1,0:T(8,128)}), s32[16,16,128]{2,1,0:T(8,128)S(1)}, u32[]{:S(2)}, u32[]{:S(2)}) async-start(s32[16,16,128]{2,1,0:T(8,128)} %get-tuple-element.14), calls=%async_computation | async-start | bytes 262144 | tf_op jit(solution)/shard_map/all_to_all | solution.py:338
  14.0 0.0 collective-permute-done.ahead_ref
  14.0 0.5 build_panel.1.refs_0_
  14.4 1.6 %collective-permute-start.3 = (bf16[336,128]{1,0:T(8,128)(2,1)S(1)}, bf16[336,128]{1,0:T(8,128)(2,1)S(1)}, u32[]{:S(2)}, u32[]{:S(2)}) collective-permute-start(bf16[336,128]{1,0:T(8,128)(2,1)S(1)} %build_panel.1.refs_0_), channel_id=1, source_target_pairs={{0,6},{1,7},{2,4},{3,5},{4,2},{5,3},{6,0},{7,1},{8,14},{9,15},{10,... | collective-permute-start | bytes 258056 | tf_op jit(solution)/shard_map/ppermute | solution.py:330
  16.0 5.0 %collective-permute-start.2 = (bf16[336,128]{1,0:T(8,128)(2,1)S(1)}, bf16[336,128]{1,0:T(8,128)(2,1)S(1)}, u32[]{:S(2)}, u32[]{:S(2)}) collective-permute-start(bf16[336,128]{1,0:T(8,128)(2,1)S(1)} %build_panel.1.refs_0_), channel_id=1, source_target_pairs={{0,4},{1,5},{2,6},{3,7},{4,0},{5,1},{6,2},{7,3},{8,12},{9,13},{10,... | collective-permute-start | bytes 258056 | tf_op jit(solution)/shard_map/ppermute | solution.py:330
  21.0 0.0 collective-permute-start.1
  21.0 0.0 collective-permute-start.4
  21.0 0.0 collective-permute-done.3.refs_3_
  21.1 0.5 collective-permute-start.7
  21.6 1.9 %collective-permute-done.2.refs_2_ = bf16[336,128]{1,0:T(8,128)(2,1)S(1)} collective-permute-done((bf16[336,128]{1,0:T(8,128)(2,1)S(1)}, bf16[336,128]{1,0:T(8,128)(2,1)S(1)}, u32[]{:S(2)}, u32[]{:S(2)}) %collective-permute-start.2) | collective-permute-done | bytes 86048 | tf_op jit(solution)/shard_map/ppermute | solution.py:330
  23.5 0.0 collective-permute-start.6
  23.5 2.0 %collective-permute-done.1.refs_1_ = bf16[336,128]{1,0:T(8,128)(2,1)S(1)} collective-permute-done((bf16[336,128]{1,0:T(8,128)(2,1)S(1)}, bf16[336,128]{1,0:T(8,128)(2,1)S(1)}, u32[]{:S(2)}, u32[]{:S(2)}) %collective-permute-start.1) | collective-permute-done | bytes 86048 | tf_op jit(solution)/shard_map/ppermute | solution.py:330
  25.5 0.0 collective-permute-start.5
  25.5 0.0 all-to-all-done.refs_8_
  25.5 0.0 collective-permute-done.4.refs_4_
  25.5 0.0 collective-permute-done.7.refs_7_
  25.5 0.0 collective-permute-done.6.refs_6_
  25.6 1.2 %collective-permute-done.5.refs_5_ = bf16[336,128]{1,0:T(8,128)(2,1)S(1)} collective-permute-done((bf16[336,128]{1,0:T(8,128)(2,1)S(1)}, bf16[336,128]{1,0:T(8,128)(2,1)S(1)}, u32[]{:S(2)}, u32[]{:S(2)}) %collective-permute-start.5) | collective-permute-done | bytes 86048 | tf_op jit(solution)/shard_map/ppermute | solution.py:330
  26.8 3.4 %contract_pairs.1 = bf16[16,112,128]{2,1,0:T(8,128)(2,1)S(1)} custom-call(bf16[336,128]{1,0:T(8,128)(2,1)S(1)} %build_panel.1.refs_0_, bf16[336,128]{1,0:T(8,128)(2,1)S(1)} %collective-permute-done.1.refs_1_, bf16[336,128]{1,0:T(8,128)(2,1)S(1)} %collective-permute-done.2.refs_2_, bf16[336,128]{1,0:T(8,128)(2,1)S(1)} %collective-permute-done.3.refs_3_, ...), custom_call_target="tpu_custom_call" | custom-call | tf_op jit(solution)/shard_map/contract_pairs/pallas_call | solution.py:285
  30.2 23.9 %all_to_all.10.refs_0_ = bf16[16,112,128]{2,1,0:T(8,128)(2,1)S(1)} all-to-all(bf16[16,112,128]{2,1,0:T(8,128)(2,1)S(1)} %contract_pairs.1), channel_id=1, replica_groups={{0,8,16,24,32,40,48,56,64,72,80,88,96,104,112,120},{1,9,17,25,33,41,49,..., dimensions={0} | all-to-all | bytes 917504 | tf_op jit(solution)/shard_map/all_to_all | solution.py:344
  54.1 0.8 %add_up.1 = f32[72,192]{1,0:T(8,128)} custom-call(bf16[16,112,128]{2,1,0:T(8,128)(2,1)S(1)} %all_to_all.10.refs_0_), custom_call_target="tpu_custom_call" | custom-call | tf_op jit(solution)/shard_map/add_up/pallas_call | solution.py:318
Async XLA Ops:
  2.0 12.0 %collective-permute-start = (bf16[6,96,256]{2,1,0:T(8,128)(2,1)S(1)}, bf16[6,96,256]{2,1,0:T(8,128)(2,1)S(1)}, u32[]{:S(2)}, u32[]{:S(2)}) collective-permute-start(bf16[6,96,256]{2,1,0:T(8,128)(2,1)S(1)} %get-tuple-element.13), channel_id=1, source_target_pairs={{0,127},{1,0},{2,1},{3,2},{4,3},{5,4},{6,5},{7,6},{8,7},{9,8},{10,... | collective-permute-start | bytes 884744 | tf_op jit(solution)/shard_map/ppermute | solution.py:337
  2.1 23.4 %all-to-all-start = ((s32[16,16,128]{2,1,0:T(8,128)}), s32[16,16,128]{2,1,0:T(8,128)S(1)}, u32[]{:S(2)}, u32[]{:S(2)}) async-start(s32[16,16,128]{2,1,0:T(8,128)} %get-tuple-element.14), calls=%async_computation | async-start | bytes 262144 | tf_op jit(solution)/shard_map/all_to_all | solution.py:338
  14.4 6.6 %collective-permute-start.3 = (bf16[336,128]{1,0:T(8,128)(2,1)S(1)}, bf16[336,128]{1,0:T(8,128)(2,1)S(1)}, u32[]{:S(2)}, u32[]{:S(2)}) collective-permute-start(bf16[336,128]{1,0:T(8,128)(2,1)S(1)} %build_panel.1.refs_0_), channel_id=1, source_target_pairs={{0,6},{1,7},{2,4},{3,5},{4,2},{5,3},{6,0},{7,1},{8,14},{9,15},{10,... | collective-permute-start | bytes 258056 | tf_op jit(solution)/shard_map/ppermute | solution.py:330
  16.0 7.5 %collective-permute-start.2 = (bf16[336,128]{1,0:T(8,128)(2,1)S(1)}, bf16[336,128]{1,0:T(8,128)(2,1)S(1)}, u32[]{:S(2)}, u32[]{:S(2)}) collective-permute-start(bf16[336,128]{1,0:T(8,128)(2,1)S(1)} %build_panel.1.refs_0_), channel_id=1, source_target_pairs={{0,4},{1,5},{2,6},{3,7},{4,0},{5,1},{6,2},{7,3},{8,12},{9,13},{10,... | collective-permute-start | bytes 258056 | tf_op jit(solution)/shard_map/ppermute | solution.py:330
  21.0 4.5 %collective-permute-start.1 = (bf16[336,128]{1,0:T(8,128)(2,1)S(1)}, bf16[336,128]{1,0:T(8,128)(2,1)S(1)}, u32[]{:S(2)}, u32[]{:S(2)}) collective-permute-start(bf16[336,128]{1,0:T(8,128)(2,1)S(1)} %build_panel.1.refs_0_), channel_id=1, source_target_pairs={{0,2},{1,3},{2,0},{3,1},{4,6},{5,7},{6,4},{7,5},{8,10},{9,11},{10,... | collective-permute-start | bytes 258056 | tf_op jit(solution)/shard_map/ppermute | solution.py:330
  21.0 4.5 %collective-permute-start.4 = (bf16[336,128]{1,0:T(8,128)(2,1)S(1)}, bf16[336,128]{1,0:T(8,128)(2,1)S(1)}, u32[]{:S(2)}, u32[]{:S(2)}) collective-permute-start(bf16[336,128]{1,0:T(8,128)(2,1)S(1)} %build_panel.1.refs_0_), channel_id=1, source_target_pairs={{0,1},{1,0},{2,3},{3,2},{4,5},{5,4},{6,7},{7,6},{8,9},{9,8},{10,11... | collective-permute-start | bytes 258056 | tf_op jit(solution)/shard_map/ppermute | solution.py:330
  21.1 4.5 %collective-permute-start.7 = (bf16[336,128]{1,0:T(8,128)(2,1)S(1)}, bf16[336,128]{1,0:T(8,128)(2,1)S(1)}, u32[]{:S(2)}, u32[]{:S(2)}) collective-permute-start(bf16[336,128]{1,0:T(8,128)(2,1)S(1)} %collective-permute-done.3.refs_3_), channel_id=1, source_target_pairs={{0,1},{1,0},{2,3},{3,2},{4,5},{5,4},{6,7},{7,6},{8,9},{9,8},{10,11... | collective-permute-start | bytes 258056 | tf_op jit(solution)/shard_map/ppermute | solution.py:330
  23.5 2.0 %collective-permute-start.6 = (bf16[336,128]{1,0:T(8,128)(2,1)S(1)}, bf16[336,128]{1,0:T(8,128)(2,1)S(1)}, u32[]{:S(2)}, u32[]{:S(2)}) collective-permute-start(bf16[336,128]{1,0:T(8,128)(2,1)S(1)} %collective-permute-done.2.refs_2_), channel_id=1, source_target_pairs={{0,1},{1,0},{2,3},{3,2},{4,5},{5,4},{6,7},{7,6},{8,9},{9,8},{10,11... | collective-permute-start | bytes 258056 | tf_op jit(solution)/shard_map/ppermute | solution.py:330
  25.5 1.3 %collective-permute-start.5 = (bf16[336,128]{1,0:T(8,128)(2,1)S(1)}, bf16[336,128]{1,0:T(8,128)(2,1)S(1)}, u32[]{:S(2)}, u32[]{:S(2)}) collective-permute-start(bf16[336,128]{1,0:T(8,128)(2,1)S(1)} %collective-permute-done.1.refs_1_), channel_id=1, source_target_pairs={{0,1},{1,0},{2,3},{3,2},{4,5},{5,4},{6,7},{7,6},{8,9},{9,8},{10,11... | collective-permute-start | bytes 258056 | tf_op jit(solution)/shard_map/ppermute | solution.py:330

commit v6 on v5

--- a/solution.py
+++ b/solution.py
@@ -15,7 +15,7 @@
 NEAR = 8
 FAR = 16
 LANES = 128
-FAR_GROUPS = [[NEAR * j + i for j in range(FAR)] for i in range(NEAR)]
+FAR_GROUPS = [[i ^ j for j in [0, 2, 4, 6, 8, 10, 12, 14, 64, 66, 68, 70, 72, 74, 76, 78]] for i in [0, 1, 16, 17, 32, 33, 48, 49]]
 PACKED = 112
 WIRE = 336
 
@@ -337,7 +337,7 @@
     ahead = lax.ppermute(plane, "gx", pairs)
     tables = lax.all_to_all(tables, "gx", 0, 0, axis_index_groups=FAR_GROUPS)
     panel = build(counts, vec, link, marks, ahead)
-    others = [swapped(panel, bits) for bits in (2, 4, 6)]
+    others = [swapped(panel, bits) for bits in (16, 48, 32)]
     panels = [panel] + others
     panels = panels + [swapped(p, 1) for p in panels]
     parts = contract(panels, tables)

time: 55.2 us -> 54.1 us (0.980); the launches traced: 55 us -> 53.2 us
  blocking collectives: 23.9 us -> 19.6 us
  starting transfers between devices: 18.4 us -> 21.2 us
    all_to_all x1, blocking collectives: 23.9 us -> 19.6 us  [shards(): parts = lax.all_to_all(parts, 'gx', 0, 0, axis_index_groups=FAR_GROUPS)]
    all_to_all x1, starting transfers between devices: 11.2 us -> 13.9 us  [shards(): tables = lax.all_to_all(tables, 'gx', 0, 0, axis_index_groups=FAR_GROUPS)]
  transfers between devices with their start and end apart: 9 -> 9, of which waited for: 3 -> 4; matrix products, arithmetic and copies ran while one was open for 0% -> 0% of each run, Pallas kernels for 1% -> 1%
where the time goes in v6:
time: 54.1 us; the launch traced here: 53.2 us
  starting transfers between devices  21.2 us (39%)
  blocking collectives  19.6 us (36%)
  Pallas kernels  6.72 us (12%)
  waiting for transfers between devices  4.9 us (9%)
  between operations  0.7 us (1%)
    all_to_all x1, blocking collectives, shards(): parts = lax.all_to_all(parts, 'gx', 0, 0, axis_index_groups=FAR_GROUPS)  19.6 us
    all_to_all x1, starting transfers between devices, shards(): tables = lax.all_to_all(tables, 'gx', 0, 0, axis_index_groups=FAR_GROUPS)  13.9 us
    ppermute x7, starting transfers between devices, swapped(): lax.ppermute(value, 'gx', [(source, source ^ bits) for source in range(co...  7.19 us
    ppermute x7, waiting for transfers between devices, swapped(): lax.ppermute(value, 'gx', [(source, source ^ bits) for source in range(co...  4.89 us
    pallas_call x1, Pallas kernels, contract(): pl.pallas_call(contract_kernel, out_shape=jax.ShapeDtypeStruct((FAR, PACK...  3.43 us
    pallas_call x1, Pallas kernels, build_local(): pl.pallas_call(local_kernel, out_shape=(pltpu.VMEM((6, MODES, PLANE), jnp...  1.98 us
  transfers between devices with their start and end apart: 9, of which 4 were waited for; matrix products, arithmetic and copies ran while one was open for 0% of the time, Pallas kernels for 1%

profile of v6, /device:TPU:2, one launch (start us, length us, event | category | flops | bytes accessed | tf_op | source)
XLA Modules:
  0.0 53.2 jit_solution(18265576333536494318)
XLA Ops:
  0.0 2.0 %local_vectors.1 = (bf16[6,96,256]{2,1,0:T(8,128)(2,1)S(1)}, s32[16,16,128]{2,1,0:T(8,128)}, f32[576,128]{1,0:T(8,128)S(1)}, f32[24,128]{1,0:T(8,128)S(1)}, s32[8,128]{1,0:T(8,128)S(1)}) custom-call(s32[1,72]{1,0:T(1,128)} %bitcast.2, s32[1,24]{1,0:T(1,128)} %bitcast.3, bf16[6,96,1024]{2,1,0:T(8,128)(2,1)} %modes_hbm.1, f32[3,18,1024]{2,1,0:T(8,128)} %links_hbm.1), custom_call_target="tpu_custom_call" | custom-call | tf_op jit(solution)/shard_map/local_vectors/pallas_call | solution.py:97
  2.0 0.1 collective-permute-start
  2.1 13.9 %all-to-all-start = ((s32[16,16,128]{2,1,0:T(8,128)}), s32[16,16,128]{2,1,0:T(8,128)S(1)}, u32[]{:S(2)}, u32[]{:S(2)}) async-start(s32[16,16,128]{2,1,0:T(8,128)} %get-tuple-element.14), calls=%async_computation | async-start | bytes 262144 | tf_op jit(solution)/shard_map/all_to_all | solution.py:338
  16.7 0.0 collective-permute-done.ahead_ref
  16.7 0.5 build_panel.1.refs_0_
  17.2 1.4 %collective-permute-start.3 = (bf16[336,128]{1,0:T(8,128)(2,1)S(1)}, bf16[336,128]{1,0:T(8,128)(2,1)S(1)}, u32[]{:S(2)}, u32[]{:S(2)}) collective-permute-start(bf16[336,128]{1,0:T(8,128)(2,1)S(1)} %build_panel.1.refs_0_), channel_id=1, source_target_pairs={{0,32},{1,33},{2,34},{3,35},{4,36},{5,37},{6,38},{7,39},{8,40},{9,... | collective-permute-start | bytes 258056 | tf_op jit(solution)/shard_map/ppermute | solution.py:330
  18.6 0.4 collective-permute-start.2
  19.0 4.8 %collective-permute-start.1 = (bf16[336,128]{1,0:T(8,128)(2,1)S(1)}, bf16[336,128]{1,0:T(8,128)(2,1)S(1)}, u32[]{:S(2)}, u32[]{:S(2)}) collective-permute-start(bf16[336,128]{1,0:T(8,128)(2,1)S(1)} %build_panel.1.refs_0_), channel_id=1, source_target_pairs={{0,16},{1,17},{2,18},{3,19},{4,20},{5,21},{6,22},{7,23},{8,24},{9,... | collective-permute-start | bytes 258056 | tf_op jit(solution)/shard_map/ppermute | solution.py:330
  23.8 0.0 collective-permute-start.4
  23.8 3.7 %collective-permute-done.3.refs_3_ = bf16[336,128]{1,0:T(8,128)(2,1)S(1)} collective-permute-done((bf16[336,128]{1,0:T(8,128)(2,1)S(1)}, bf16[336,128]{1,0:T(8,128)(2,1)S(1)}, u32[]{:S(2)}, u32[]{:S(2)}) %collective-permute-start.3) | collective-permute-done | bytes 86048 | tf_op jit(solution)/shard_map/ppermute | solution.py:330
  27.5 0.0 collective-permute-start.7
  27.5 0.0 collective-permute-done.2.refs_2_
  27.5 0.5 collective-permute-start.6
  28.0 0.0 collective-permute-done.1.refs_1_
  28.0 0.1 collective-permute-start.5
  28.1 0.0 all-to-all-done.refs_8_
  28.1 0.0 collective-permute-done.4.refs_4_
  28.1 0.7 %collective-permute-done.7.refs_7_ = bf16[336,128]{1,0:T(8,128)(2,1)S(1)} collective-permute-done((bf16[336,128]{1,0:T(8,128)(2,1)S(1)}, bf16[336,128]{1,0:T(8,128)(2,1)S(1)}, u32[]{:S(2)}, u32[]{:S(2)}) %collective-permute-start.7) | collective-permute-done | bytes 86048 | tf_op jit(solution)/shard_map/ppermute | solution.py:330
  28.7 0.2 collective-permute-done.6.refs_6_
  28.9 0.4 collective-permute-done.5.refs_5_
  29.3 3.4 %contract_pairs.1 = bf16[16,112,128]{2,1,0:T(8,128)(2,1)S(1)} custom-call(bf16[336,128]{1,0:T(8,128)(2,1)S(1)} %build_panel.1.refs_0_, bf16[336,128]{1,0:T(8,128)(2,1)S(1)} %collective-permute-done.1.refs_1_, bf16[336,128]{1,0:T(8,128)(2,1)S(1)} %collective-permute-done.2.refs_2_, bf16[336,128]{1,0:T(8,128)(2,1)S(1)} %collective-permute-done.3.refs_3_, ...), custom_call_target="tpu_custom_call" | custom-call | tf_op jit(solution)/shard_map/contract_pairs/pallas_call | solution.py:285
  32.7 19.6 %all_to_all.10.refs_0_ = bf16[16,112,128]{2,1,0:T(8,128)(2,1)S(1)} all-to-all(bf16[16,112,128]{2,1,0:T(8,128)(2,1)S(1)} %contract_pairs.1), channel_id=1, replica_groups={{0,2,4,6,8,10,12,14,64,66,68,70,72,74,76,78},{1,3,5,7,9,11,13,15,65,67,..., dimensions={0} | all-to-all | bytes 917504 | tf_op jit(solution)/shard_map/all_to_all | solution.py:344
  52.3 0.8 %add_up.1 = f32[72,192]{1,0:T(8,128)} custom-call(bf16[16,112,128]{2,1,0:T(8,128)(2,1)S(1)} %all_to_all.10.refs_0_), custom_call_target="tpu_custom_call" | custom-call | tf_op jit(solution)/shard_map/add_up/pallas_call | solution.py:318
Async XLA Ops:
  2.0 14.7 %collective-permute-start = (bf16[6,96,256]{2,1,0:T(8,128)(2,1)S(1)}, bf16[6,96,256]{2,1,0:T(8,128)(2,1)S(1)}, u32[]{:S(2)}, u32[]{:S(2)}) collective-permute-start(bf16[6,96,256]{2,1,0:T(8,128)(2,1)S(1)} %get-tuple-element.13), channel_id=1, source_target_pairs={{0,127},{1,0},{2,1},{3,2},{4,3},{5,4},{6,5},{7,6},{8,7},{9,8},{10,... | collective-permute-start | bytes 884744 | tf_op jit(solution)/shard_map/ppermute | solution.py:337
  2.1 26.0 %all-to-all-start = ((s32[16,16,128]{2,1,0:T(8,128)}), s32[16,16,128]{2,1,0:T(8,128)S(1)}, u32[]{:S(2)}, u32[]{:S(2)}) async-start(s32[16,16,128]{2,1,0:T(8,128)} %get-tuple-element.14), calls=%async_computation | async-start | bytes 262144 | tf_op jit(solution)/shard_map/all_to_all | solution.py:338
  17.2 10.3 %collective-permute-start.3 = (bf16[336,128]{1,0:T(8,128)(2,1)S(1)}, bf16[336,128]{1,0:T(8,128)(2,1)S(1)}, u32[]{:S(2)}, u32[]{:S(2)}) collective-permute-start(bf16[336,128]{1,0:T(8,128)(2,1)S(1)} %build_panel.1.refs_0_), channel_id=1, source_target_pairs={{0,32},{1,33},{2,34},{3,35},{4,36},{5,37},{6,38},{7,39},{8,40},{9,... | collective-permute-start | bytes 258056 | tf_op jit(solution)/shard_map/ppermute | solution.py:330
  18.6 8.9 %collective-permute-start.2 = (bf16[336,128]{1,0:T(8,128)(2,1)S(1)}, bf16[336,128]{1,0:T(8,128)(2,1)S(1)}, u32[]{:S(2)}, u32[]{:S(2)}) collective-permute-start(bf16[336,128]{1,0:T(8,128)(2,1)S(1)} %build_panel.1.refs_0_), channel_id=1, source_target_pairs={{0,48},{1,49},{2,50},{3,51},{4,52},{5,53},{6,54},{7,55},{8,56},{9,... | collective-permute-start | bytes 258056 | tf_op jit(solution)/shard_map/ppermute | solution.py:330
  19.0 9.0 %collective-permute-start.1 = (bf16[336,128]{1,0:T(8,128)(2,1)S(1)}, bf16[336,128]{1,0:T(8,128)(2,1)S(1)}, u32[]{:S(2)}, u32[]{:S(2)}) collective-permute-start(bf16[336,128]{1,0:T(8,128)(2,1)S(1)} %build_panel.1.refs_0_), channel_id=1, source_target_pairs={{0,16},{1,17},{2,18},{3,19},{4,20},{5,21},{6,22},{7,23},{8,24},{9,... | collective-permute-start | bytes 258056 | tf_op jit(solution)/shard_map/ppermute | solution.py:330
  23.8 4.3 %collective-permute-start.4 = (bf16[336,128]{1,0:T(8,128)(2,1)S(1)}, bf16[336,128]{1,0:T(8,128)(2,1)S(1)}, u32[]{:S(2)}, u32[]{:S(2)}) collective-permute-start(bf16[336,128]{1,0:T(8,128)(2,1)S(1)} %build_panel.1.refs_0_), channel_id=1, source_target_pairs={{0,1},{1,0},{2,3},{3,2},{4,5},{5,4},{6,7},{7,6},{8,9},{9,8},{10,11... | collective-permute-start | bytes 258056 | tf_op jit(solution)/shard_map/ppermute | solution.py:330
  27.5 1.3 %collective-permute-start.7 = (bf16[336,128]{1,0:T(8,128)(2,1)S(1)}, bf16[336,128]{1,0:T(8,128)(2,1)S(1)}, u32[]{:S(2)}, u32[]{:S(2)}) collective-permute-start(bf16[336,128]{1,0:T(8,128)(2,1)S(1)} %collective-permute-done.3.refs_3_), channel_id=1, source_target_pairs={{0,1},{1,0},{2,3},{3,2},{4,5},{5,4},{6,7},{7,6},{8,9},{9,8},{10,11... | collective-permute-start | bytes 258056 | tf_op jit(solution)/shard_map/ppermute | solution.py:330
  27.5 1.4 %collective-permute-start.6 = (bf16[336,128]{1,0:T(8,128)(2,1)S(1)}, bf16[336,128]{1,0:T(8,128)(2,1)S(1)}, u32[]{:S(2)}, u32[]{:S(2)}) collective-permute-start(bf16[336,128]{1,0:T(8,128)(2,1)S(1)} %collective-permute-done.2.refs_2_), channel_id=1, source_target_pairs={{0,1},{1,0},{2,3},{3,2},{4,5},{5,4},{6,7},{7,6},{8,9},{9,8},{10,11... | collective-permute-start | bytes 258056 | tf_op jit(solution)/shard_map/ppermute | solution.py:330
  28.0 1.3 %collective-permute-start.5 = (bf16[336,128]{1,0:T(8,128)(2,1)S(1)}, bf16[336,128]{1,0:T(8,128)(2,1)S(1)}, u32[]{:S(2)}, u32[]{:S(2)}) collective-permute-start(bf16[336,128]{1,0:T(8,128)(2,1)S(1)} %collective-permute-done.1.refs_1_), channel_id=1, source_target_pairs={{0,1},{1,0},{2,3},{3,2},{4,5},{5,4},{6,7},{7,6},{8,9},{9,8},{10,11... | collective-permute-start | bytes 258056 | tf_op jit(solution)/shard_map/ppermute | solution.py:330
